TPU v7x, 1024 devices: a whole 8x8x8 slice. The times are simulated.
1024 devices in a mesh: chan: 16 (over x, y_hi), ctx: 64 (over z, y_lo, core).
Axes of the slice: x: 8, y: 8 (y_hi: 2, y_lo: 4; y = y_hi * 4 + y_lo), z: 8, core: 2. Of those that a mesh axis runs over, the one named last changes fastest.
Arguments:
- short_query: bfloat16 [4096, 65536], P('chan', 'ctx'), may hold values from -6 to 6
- short_key: bfloat16 [4096, 65536], P('chan', 'ctx'), may hold values from -6 to 6
- short_value: bfloat16 [4096, 65536], P('chan', 'ctx'), may hold values from -6 to 6
- long_query: bfloat16 [4096, 65536], P('chan', 'ctx'), may hold values from -6 to 6
- long_key: bfloat16 [4096, 65536], P('chan', 'ctx'), may hold values from -6 to 6
- short_taps: bfloat16 [256, 128], P('chan'), may hold values from -0.5 to 0.5
- long_residue: float32 [256, 16], P('chan'), may hold values from -2 to 2
- long_rate: float32 [256, 16], P('chan'), may hold values from 3e-06 to 0.05
Outputs:
- block_output: bfloat16 [4096, 65536], P('chan', 'ctx')
All inputs are finite; a program needn't handle non-finite values.
Results may differ from a plain program's by a relative error of at most 0.015.
Values may be sent and summed in bfloat16 or wider, within the bound.
A program may use at most 64 MiB of HBM per device.

v0:
```python
import jax
import jax.numpy as jnp
from jax import lax
from jax.sharding import PartitionSpec as P

TAPS = 128
FGROUP = 16


def shifted(shard, axis, by):
    count = lax.axis_size(axis)
    pairs = [(i, i + by) for i in range(count) if 0 <= i + by < count]
    return lax.ppermute(shard, axis, pairs)


def skewed(line):
    count = line.shape[0]
    reverse = jnp.flip(line, axis=1)
    tiled = jnp.tile(reverse, (1, TAPS))
    rows = tiled[:, : TAPS * (2 * TAPS - 1)].reshape(count, TAPS, 2 * TAPS - 1)
    return rows[:, :, TAPS - 1 : 2 * TAPS - 1]


def lower_toeplitz(taps):
    padded = jnp.concatenate([jnp.zeros_like(taps), taps], axis=1)
    return skewed(padded)


def upper_toeplitz(taps):
    padded = jnp.concatenate([taps, jnp.zeros_like(taps)], axis=1)
    return skewed(padded)


def short_conv(mixed, taps, lower, upper):
    chans, length = mixed.shape
    count = length // TAPS
    half = count // 2
    blocks = mixed.reshape(chans, count, TAPS)
    previous = jnp.concatenate(
        [lower[:, None], blocks[:, : half - 1], upper[:, None], blocks[:, half : count - 1]], axis=1
    )
    groups = chans // FGROUP
    blocks = blocks.reshape(groups, FGROUP, count, TAPS)
    previous = previous.reshape(groups, FGROUP, count, TAPS)
    result = jnp.einsum(
        "gts,gcms->gcmt", lower_toeplitz(taps), blocks, preferred_element_type=jnp.float32
    )
    result = result + jnp.einsum(
        "gts,gcms->gcmt", upper_toeplitz(taps), previous, preferred_element_type=jnp.float32
    )
    return result.reshape(chans, length)


def split_float(values):
    high_part = values.astype(jnp.bfloat16)
    low_part = (values - high_part.astype(jnp.float32)).astype(jnp.bfloat16)
    return (high_part, low_part)


def filter_dot(form, filt, data):
    high_part, low_part = split_float(filt)
    result = jnp.einsum(form, high_part, data, preferred_element_type=jnp.float32)
    return result + jnp.einsum(form, low_part, data, preferred_element_type=jnp.float32)


def state_dot(form, filt, states):
    filt_high, filt_low = split_float(filt)
    state_high, state_low = split_float(states)
    result = jnp.einsum(form, filt_high, state_high, preferred_element_type=jnp.float32)
    result = result + jnp.einsum(form, filt_low, state_high, preferred_element_type=jnp.float32)
    return result + jnp.einsum(form, filt_high, state_low, preferred_element_type=jnp.float32)


def filter_parts(rate, residue):
    places = jnp.arange(TAPS, dtype=jnp.float32)
    weight = residue * jnp.sqrt(rate)
    taps = jnp.sum(weight[:, :, None] * jnp.exp(-rate[:, :, None] * places), axis=1)
    to_end = jnp.exp(-rate[:, :, None] * (TAPS - 1.0 - places))
    from_start = weight[:, :, None] * jnp.exp(-rate[:, :, None] * (places + 1.0))
    return (lower_toeplitz(taps), to_end, from_start)


def block_conv(blocks, parts, rate):
    toeplitz, to_end, from_start = parts
    inner = filter_dot("gts,gcms->gcmt", toeplitz, blocks)
    ends = filter_dot("gns,gcms->gcmn", to_end, blocks)
    decay = TAPS * rate[:, None, None, :]
    counter = jnp.ones((1, 1, ends.shape[2], 1), jnp.float32)

    def combine(early, late):
        return (early[0] * jnp.exp(-decay * late[1]) + late[0], early[1] + late[1])

    prefix, _ = lax.associative_scan(combine, (ends, counter), axis=2)
    starts = jnp.concatenate([jnp.zeros_like(prefix[:, :, :1]), prefix[:, :, :-1]], axis=2)
    carried = state_dot("gnt,gcmn->gcmt", from_start, starts)
    return (inner + carried, prefix[:, :, -1])


def per_device(
    short_query, short_key, short_value, long_query, long_key, short_taps, long_residue, long_rate
):
    chans, length = short_key.shape
    half = length // 2
    mixed = (short_key.astype(jnp.float32) * short_value.astype(jnp.float32)).astype(jnp.bfloat16)
    lower = shifted(mixed[:, half - TAPS : half], "ctx", 1)
    upper = shifted(mixed[:, length - TAPS :], "ctx", -1)
    is_last = lax.axis_index("ctx") == lax.axis_size("ctx") - 1
    upper = jnp.where(is_last, mixed[:, half - TAPS : half], upper)
    short_out = short_conv(mixed, short_taps, lower, upper)
    long_input = (
        long_key.astype(jnp.float32) * (short_query.astype(jnp.float32) * short_out)
    ).astype(jnp.bfloat16)
    devices = lax.axis_size("ctx")
    piece = chans // devices
    regrouped = lax.all_to_all(long_input, "ctx", split_axis=0, concat_axis=1, tiled=True)
    split = regrouped.reshape(piece, devices, 2, half)
    ordered = jnp.concatenate(
        [
            split[:, :, 0].reshape(piece, devices * half),
            jnp.flip(split[:, :, 1], axis=1).reshape(piece, devices * half),
        ],
        axis=1,
    )
    piece_groups = max(piece // FGROUP, 1)
    per_group = piece // piece_groups
    first_group = lax.axis_index("ctx") * piece // FGROUP
    rate = lax.dynamic_slice_in_dim(long_rate, first_group, piece_groups, 0)
    residue = lax.dynamic_slice_in_dim(long_residue, first_group, piece_groups, 0)
    parts = filter_parts(rate, residue)
    total = devices * length
    result, _ = block_conv(
        ordered.reshape(piece_groups, per_group, total // TAPS, TAPS), parts, rate
    )
    result = result.reshape(piece, 2 * devices, half)
    restored = jnp.stack(
        [result[:, :devices], jnp.flip(result[:, devices:], axis=1)], axis=2
    ).reshape(piece, total)
    long_out = lax.all_to_all(restored, "ctx", split_axis=1, concat_axis=0, tiled=True)
    return (long_query.astype(jnp.float32) * long_out).astype(jnp.bfloat16)


def solution(mesh):
    in_specs = (
        P("chan", "ctx"),
        P("chan", "ctx"),
        P("chan", "ctx"),
        P("chan", "ctx"),
        P("chan", "ctx"),
        P("chan", None),
        P("chan", None),
        P("chan", None),
    )
    out_specs = P("chan", "ctx")
    return jax.shard_map(
        per_device, mesh=mesh, in_specs=in_specs, out_specs=out_specs, check_vma=False
    )
```

profile of v0, /device:TPU:1, one launch (start us, length us, event | category | flops | bytes accessed | tf_op | source)
XLA Modules:
  0.0 139.7 jit_solution(7913946555799472436)
XLA Ops:
  0.0 1.4 multiply_convert_fusion.1
  1.4 16.1 %collective-permute-start.1 = (bf16[256,128]{1,0:T(8,128)(2,1)S(1)}, bf16[256,128]{1,0:T(8,128)(2,1)S(1)}, u32[]{:S(2)}, u32[]{:S(2)}) collective-permute-start(bf16[256,128]{1,0:T(8,128)(2,1)S(1)} %slice.237), channel_id=1, source_target_pairs={{1,0},{2,1},{3,2},{4,3},{5,4},{6,5},{7,6},{8,7},{9,8},{10,9},{11,1... | collective-permute-start | bytes 196616 | tf_op jit(solution)/shard_map/ppermute | solution.py:13
  17.6 0.6 copy-done.6
  18.4 0.6 copy.45
  19.1 3.4 %reshape.712 = bf16[16,128,255]{2,1,0:T(8,128)(2,1)S(1)} reshape(bf16[16,32640]{1,0:T(8,128)(2,1)S(1)} %slice.233) | data formatting | bytes 2088960 | tf_op jit(solution)/shard_map/reshape | solution.py:20
  22.5 0.6 fusion.4
  23.1 0.6 fusion.60
  23.7 1.9 %collective-permute-start = (bf16[256,128]{1,0:T(8,128)(2,1)}, bf16[256,128]{1,0:T(8,128)(2,1)S(1)}, u32[]{:S(2)}, u32[]{:S(2)}) collective-permute-start(bf16[256,128]{1,0:T(8,128)(2,1)} %get-tuple-element.11), channel_id=1, source_target_pairs={{0,1},{1,2},{2,3},{3,4},{4,5},{5,6},{6,7},{7,8},{8,9},{9,10},{10,1... | collective-permute-start | bytes 196616 | tf_op jit(solution)/shard_map/ppermute | solution.py:13
  25.6 0.9 fusion.61
  26.7 0.6 copy.47
  27.4 3.4 %reshape.714 = bf16[16,128,255]{2,1,0:T(8,128)(2,1)S(1)} reshape(bf16[16,32640]{1,0:T(8,128)(2,1)S(1)} %slice.239) | data formatting | bytes 2088960 | tf_op jit(solution)/shard_map/reshape | solution.py:20
  31.0 0.7 copy-done
  31.7 0.9 convolution_add_fusion.2
  32.9 0.4 fusion.3
  33.4 1.0 all_to_all.26
  34.3 10.9 %all-to-all-start = ((bf16[64,4,1024]{2,1,0:T(4,128)(2,1)}), bf16[64,4,1024]{2,1,0:T(4,128)(2,1)S(1)}, u32[]{:S(2)}, u32[]{:S(2)}) async-start(bf16[64,4,1024]{2,1,0:T(4,128)(2,1)} %all_to_all.26), calls=%async_computation | async-start | bytes 1048576 | tf_op jit(solution)/shard_map/all_to_all | solution.py:115
  45.3 0.7 exponential_bitcast_fusion
  46.5 0.3 slice_reduce_fusion.1
  46.8 0.3 reshape.717
  47.2 16.6 %all-to-all-done = bf16[64,4,1024]{2,1,0:T(4,128)(2,1)S(1)} async-done(((bf16[64,4,1024]{2,1,0:T(4,128)(2,1)}), bf16[64,4,1024]{2,1,0:T(4,128)(2,1)S(1)}, u32[]{:S(2)}, u32[]{:S(2)}) %all-to-all-start) | async-done | bytes 524320 | tf_op jit(solution)/shard_map/all_to_all | solution.py:115
  64.0 1.9 %fusion.59 = (bf16[4,64,1,512]{3,2,0,1:T(2,128)(2,1)S(1)}, bf16[4,64,512]{2,0,1:T(4,128)(2,1)S(1)}) fusion(bf16[4,64,2,512]{3,2,0,1:T(2,128)(2,1)S(1)} %reshape.731), kind=kLoop, calls=%fused_computation.120 | loop fusion | bytes 1048576 | tf_op jit(solution)/shard_map/slice | solution.py:120
  67.0 0.3 fusion.1
  67.3 2.2 %slice.189 = f32[1,4,256,16]{2,3,1,0:T(8,128)S(1)} slice(f32[1,4,512,16]{2,3,1,0:T(8,128)S(1)} %fusion.1), slice={[0:1:1], [0:4:1], [0:511:2], [0:16:1]} | slice | bytes 131072 | tf_op jit(solution)/shard_map/slice | solution.py:93
  69.5 2.2 %slice.190 = f32[1,4,256,16]{2,3,1,0:T(8,128)S(1)} slice(f32[1,4,512,16]{2,3,1,0:T(8,128)S(1)} %fusion.1), slice={[0:1:1], [0:4:1], [1:512:2], [0:16:1]} | slice | bytes 131072 | tf_op jit(solution)/shard_map/slice | solution.py:93
  71.8 1.1 slice.192
  73.0 1.1 slice.193
  74.2 0.6 slice.195
  74.8 0.6 slice.196
  75.5 0.3 slice.198
  75.8 0.3 slice.199
  78.4 0.3 slice.223
  78.7 0.6 slice.225
  79.3 1.1 slice.227
  80.4 2.2 %slice.229 = f32[1,4,255,16]{2,3,1,0:T(8,128)S(1)} slice(f32[1,4,512,16]{2,3,1,0:T(8,128)S(1)} %fusion.1), slice={[0:1:1], [0:4:1], [2:512:2], [0:16:1]} | slice | bytes 130560 | tf_op jit(solution)/shard_map/slice | solution.py:93
  83.3 0.3 pad.64
  83.8 0.3 pad.63
  84.3 0.3 pad.65
  84.6 0.3 pad.66
  85.0 0.4 pad.68
  85.5 0.4 pad.67
  86.1 0.5 pad.69
  86.6 0.5 pad.70
  87.2 0.8 pad.72
  88.2 0.8 pad.71
  89.1 0.7 slice-done.1
  89.8 1.3 pad.73
  91.2 1.3 pad.74
  92.5 2.4 %pad.140 = f32[1,4,512,16]{2,3,1,0:T(8,128)S(1)} pad(f32[1,4,256,16]{2,3,1,0:T(8,128)S(1)} %add.190, f32[]{:T(128)} %constant.9.clone.1), padding=0_0_0x0_0_0x1_0_1x0_0_0 | pad | bytes 196612
  95.0 0.7 slice-done
  95.8 2.6 %pad.100 = f32[1,4,511,16]{2,3,1,0:T(8,128)S(1)} pad(f32[1,4,256,16]{2,3,1,0:T(8,128)S(1)} %pad_maximum_fusion.1, f32[]{:T(128)} %constant.9.clone.1), padding=0_0_0x0_0_0x0_0_1x0_0_0 | pad | bytes 196356 | tf_op jit(solution)/shard_map/slice | solution.py:94
  98.5 0.5 fusion.28
  98.9 0.5 convolution_add_fusion.1
  99.4 0.4 fusion.25
  99.8 0.4 convolution_add_fusion.3
  100.1 0.5 fusion
  101.1 0.4 stack.10
  101.4 0.5 copy.32
  102.0 0.9 pad_maximum_fusion
  102.9 0.9 all_to_all.29
  103.8 0.7 copy.33
  104.5 33.2 %all_to_all.35 = f32[4,64,1024]{2,0,1:T(4,128)S(1)} all-to-all(f32[4,64,1024]{2,0,1:T(4,128)S(1)} %copy.33), channel_id=1, replica_groups=mesh['chan'=16,'ctx'=64] {'ctx'}, dimensions={1} | all-to-all | bytes 2097152 | tf_op jit(solution)/shard_map/all_to_all | solution.py:138
  137.7 0.4 all_to_all.32
  138.1 0.7 copy-done.5
  138.8 0.9 multiply_convert_fusion
  (93 shorter events, 7.6 us)
Async XLA Ops:
  1.4 21.6 %collective-permute-start.1 = (bf16[256,128]{1,0:T(8,128)(2,1)S(1)}, bf16[256,128]{1,0:T(8,128)(2,1)S(1)}, u32[]{:S(2)}, u32[]{:S(2)}) collective-permute-start(bf16[256,128]{1,0:T(8,128)(2,1)S(1)} %slice.237), channel_id=1, source_target_pairs={{1,0},{2,1},{3,2},{4,3},{5,4},{6,5},{7,6},{8,7},{9,8},{10,9},{11,1... | collective-permute-start | bytes 196616 | tf_op jit(solution)/shard_map/ppermute | solution.py:13
  17.5 0.7 copy-start.6
  23.7 7.2 %collective-permute-start = (bf16[256,128]{1,0:T(8,128)(2,1)}, bf16[256,128]{1,0:T(8,128)(2,1)S(1)}, u32[]{:S(2)}, u32[]{:S(2)}) collective-permute-start(bf16[256,128]{1,0:T(8,128)(2,1)} %get-tuple-element.11), channel_id=1, source_target_pairs={{0,1},{1,2},{2,3},{3,4},{4,5},{5,6},{6,7},{7,8},{8,9},{9,10},{10,1... | collective-permute-start | bytes 196616 | tf_op jit(solution)/shard_map/ppermute | solution.py:13
  30.8 1.0 copy-start
  31.7 1.0 copy-start.3
  31.7 1.2 copy-start.4
  34.3 29.4 %all-to-all-start = ((bf16[64,4,1024]{2,1,0:T(4,128)(2,1)}), bf16[64,4,1024]{2,1,0:T(4,128)(2,1)S(1)}, u32[]{:S(2)}, u32[]{:S(2)}) async-start(bf16[64,4,1024]{2,1,0:T(4,128)(2,1)} %all_to_all.26), calls=%async_computation | async-start | bytes 1048576 | tf_op jit(solution)/shard_map/all_to_all | solution.py:115
  67.3 15.3 %copy-start.1 = (f32[1,4,512,16]{2,3,1,0:T(8,128)}, f32[1,4,512,16]{2,3,1,0:T(8,128)S(1)}, u32[]{:S(2)}) copy-start(f32[1,4,512,16]{2,3,1,0:T(8,128)S(1)} %fusion.1) | copy-start | bytes 393220
  71.8 8.6 %copy-start.2 = (f32[1,4,256,16]{2,3,1,0:T(8,128)}, f32[1,4,256,16]{2,3,1,0:T(8,128)S(1)}, u32[]{:S(2)}) copy-start(f32[1,4,256,16]{2,3,1,0:T(8,128)S(1)} %multiply_add_fusion) | copy-start | bytes 196612
  89.0 0.8 slice-start.1
  94.9 0.8 slice-start
  137.7 1.0 copy-start.5
where the time goes:
time: 140 us
  local copies, waits for them, and re-layouts  48.9 us (35%)
  blocking collectives  33.2 us (24%)
  starting transfers between devices  28.9 us (21%)
  waiting for transfers between devices  16.6 us (12%)
  other arithmetic  7.28 us (5%)
  matrix products  4.17 us (3%)
    all_to_all x1, blocking collectives, per_device(): lax.all_to_all(restored, 'ctx', split_axis=1, concat_axis=0, tiled=True)  33.2 us
    ppermute x2, starting transfers between devices, shifted(): return lax.ppermute(shard, axis, pairs)  18 us
    all_to_all x1, waiting for transfers between devices, per_device(): lax.all_to_all(long_input, 'ctx', split_axis=0, concat_axis=1, tiled=True)  16.6 us
    slice x27, local copies, waits for them, and re-layouts, block_conv(): prefix, _ = lax.associative_scan(combine, (ends, counter), axis=2)  15.7 us
    all_to_all x1, starting transfers between devices, per_device(): lax.all_to_all(long_input, 'ctx', split_axis=0, concat_axis=1, tiled=True)  10.9 us
    pad x14, local copies, waits for them, and re-layouts, block_conv(): prefix, _ = lax.associative_scan(combine, (ends, counter), axis=2)  7.98 us
    reshape x3, local copies, waits for them, and re-layouts, skewed(): rows = tiled[:, :TAPS * (2 * TAPS - 1)].reshape(count, TAPS, 2 * TAPS - 1)  7.05 us
    unnamed x23, local copies, waits for them, and re-layouts  6.33 us
  transfers between devices with their start and end apart: 3, of which 1 were waited for; matrix products, arithmetic and copies ran while one was open for 9% of the time, Pallas kernels for 0%

commit v1 on v0

v1 whole, which is shorter than its diff:
```python
import functools

import jax
import jax.numpy as jnp
from jax import lax
from jax.experimental import pallas as pl
from jax.experimental.pallas import tpu as pltpu
from jax.sharding import PartitionSpec as P

TAPS = 128
FGROUP = 16
MODES = 16
CHUNK = 256
RING = 8
LANES = 128
MESH = pl.DeviceIdType.MESH
F32 = jnp.float32
BF16 = jnp.bfloat16


def dot(a, b):
    return lax.dot_general(a, b, (((1,), (0,)), ((), ())), preferred_element_type=F32)


def dot_t(a, b):
    return lax.dot_general(a, b, (((1,), (1,)), ((), ())), preferred_element_type=F32)


def split_float(values):
    high = values.astype(BF16)
    low = (values - high.astype(F32)).astype(BF16)
    return high, low


def iota(shape, axis):
    return lax.broadcasted_iota(jnp.int32, shape, axis)


def kernel(
    n_ctx,
    sq_hbm,
    sk_hbm,
    sv_hbm,
    lq_hbm,
    lk_hbm,
    taps_hbm,
    res_hbm,
    rate_hbm,
    out,
    sq,
    sk,
    sv,
    lq,
    lk,
    taps,
    res,
    rate,
    mixed,
    tails,
    halo,
    first,
    upper_w,
    taps_f,
    pad,
    fe,
    gt,
    filt,
    x,
    y,
    ends,
    e_out,
    e_in,
    p_out,
    p_in,
    s_out,
    s_in,
    coef,
    load_sem,
    halo_send,
    halo_recv,
    a_send,
    a_recv,
    b_send,
    b_recv,
    c_send,
    c_recv,
):
    chans, length = sk.shape
    half = length // 2
    groups = chans // FGROUP
    nz = n_ctx // RING
    me = lax.axis_index("ctx")
    plane = lax.div(me, RING)
    place = lax.rem(me, RING)
    after = lax.rem(me + 1, n_ctx)
    before = lax.rem(me + n_ctx - 1, n_ctx)

    def in_plane(k):
        return plane * RING + lax.rem(place + k, RING)

    def in_column(k):
        return lax.rem(plane + k, nz) * RING + place

    def load(n, src, dst):
        copy = pltpu.make_async_copy(src, dst, load_sem.at[n])
        copy.start()
        return copy

    tail_cols = ((half - TAPS, half), (length - TAPS, length))
    body_cols = ((0, half - TAPS), (half, length - TAPS))
    tail_loads = []
    for b, (lo, hi) in enumerate(tail_cols):
        tail_loads.append(load(2 * b, sk_hbm.at[:, lo:hi], sk.at[:, lo:hi]))
        tail_loads.append(load(2 * b + 1, sv_hbm.at[:, lo:hi], sv.at[:, lo:hi]))
    rate_load = load(4, rate_hbm, rate)
    res_load = load(5, res_hbm, res)
    taps_load = load(6, taps_hbm, taps)
    body_loads = []
    for b, (lo, hi) in enumerate(body_cols):
        body_loads.append(load(7 + 2 * b, sk_hbm.at[:, lo:hi], sk.at[:, lo:hi]))
        body_loads.append(load(8 + 2 * b, sv_hbm.at[:, lo:hi], sv.at[:, lo:hi]))
    sq_load = load(11, sq_hbm, sq)
    lk_load = load(12, lk_hbm, lk)
    lq_load = load(13, lq_hbm, lq)

    barrier = pltpu.get_barrier_semaphore()
    partners = [before, after]
    partners += [in_plane(k) for k in range(1, RING)]
    partners += [in_column(k) for k in range(1, nz)]
    for partner in partners:
        pl.semaphore_signal(
            barrier, inc=1, device_id={"ctx": partner}, device_id_type=MESH
        )

    for copy in tail_loads:
        copy.wait()
    for b, (lo, hi) in enumerate(tail_cols):
        product = sk[:, lo:hi] * sv[:, lo:hi]
        mixed[:, lo:hi] = product
        tails[b] = product
    pl.semaphore_wait(barrier, len(partners))

    halo_copies = []
    for b, target in enumerate((after, before)):
        copy = pltpu.make_async_remote_copy(
            src_ref=tails.at[b],
            dst_ref=halo.at[b],
            send_sem=halo_send.at[b],
            recv_sem=halo_recv.at[b],
            device_id={"ctx": target},
            device_id_type=MESH,
        )
        copy.start()
        halo_copies.append(copy)

    rate_load.wait()
    res_load.wait()
    taps_load.wait()
    taps_f[...] = taps[...].astype(F32)

    def spread(values):
        pad[...] = jnp.zeros_like(pad)
        pad[:, 0:MODES] = values
        return pltpu.roll(pad[...], 0, 1, stride=MODES, stride_axis=0)

    rate_row = jnp.sum(spread(rate[...]), axis=0, keepdims=True)
    weight = spread(res[...] * jnp.sqrt(rate[...]))
    weight_row = jnp.sum(weight, axis=0, keepdims=True)
    steps = iota((CHUNK, LANES), 0).astype(F32)
    for h in range(2):
        r = rate_row[:, h * LANES : (h + 1) * LANES]
        high, low = split_float(jnp.exp(-r * steps))
        gt[h, :, 0:LANES] = high
        gt[h, :, LANES:] = low
        high, low = split_float(jnp.exp(-r * (CHUNK - 1.0 - steps)))
        fe[h, :, 0:LANES] = high
        fe[h, :, LANES:] = low

    total = jnp.zeros((groups, CHUNK), F32)
    for h in range(2):
        high, low = split_float(weight[:, h * LANES : (h + 1) * LANES])
        total = total + dot_t(jnp.concatenate([high, high], axis=1), gt[h])
        total = total + dot_t(
            jnp.concatenate([low, jnp.zeros_like(low)], axis=1), gt[h]
        )
    filt[...] = total

    for copy in body_loads:
        copy.wait()
    for lo, hi in body_cols:
        mixed[:, lo:hi] = sk[:, lo:hi] * sv[:, lo:hi]
    sq_load.wait()
    lk_load.wait()

    lower_mask = iota((TAPS, TAPS), 1) >= iota((TAPS, TAPS), 0)
    blocks = length // TAPS
    firsts = (0, blocks // 2)

    def gated(rows, m, conv):
        cols = pl.ds(m * TAPS, TAPS)
        value = lk[rows, cols].astype(F32) * (sq[rows, cols].astype(F32) * conv)
        x[rows, cols] = value.astype(BF16)

    def short_group(g, _):
        rows = pl.ds(pl.multiple_of(g * FGROUP, FGROUP), FGROUP)
        line = jnp.broadcast_to(taps_f[pl.ds(g, 1), :], (TAPS, TAPS))
        skew = pltpu.roll(line, 0, 1, stride=1, stride_axis=0)
        upper = jnp.where(lower_mask, 0.0, skew).astype(BF16)
        lower = jnp.where(lower_mask, skew, 0.0).astype(BF16)
        upper_w[g] = upper
        data = []
        for m in range(blocks):
            if m in firsts:
                here = mixed[rows, m * TAPS : (m + 1) * TAPS]
                data.append(jnp.concatenate([jnp.zeros_like(here), here], axis=1))
            else:
                data.append(mixed[rows, (m - 1) * TAPS : (m + 1) * TAPS])
        conv = dot(
            jnp.concatenate(data, axis=0), jnp.concatenate([upper, lower], axis=0)
        )
        for m in range(blocks):
            part = conv[m * FGROUP : (m + 1) * FGROUP]
            if m in firsts:
                first[firsts.index(m), rows, :] = part
            else:
                gated(rows, m, part)
        return 0

    lax.fori_loop(0, groups, short_group, 0, unroll=4)

    diag = lax.div(iota((LANES, LANES), 0), FGROUP) == lax.div(
        iota((LANES, LANES), 1), MODES
    )

    def chunk_ends(chunk):
        for h in range(2):
            both = dot(
                x[h * LANES : (h + 1) * LANES, chunk * CHUNK : (chunk + 1) * CHUNK],
                fe[h],
            )
            own = jnp.where(diag, both[:, 0:LANES] + both[:, LANES:], 0.0)
            ends[chunk, :, h * LANES : (h + 1) * LANES] = jnp.sum(
                own.reshape(LANES // FGROUP, FGROUP, LANES), axis=0
            )

    chunk_ends(1)
    chunk_ends(3)

    for copy in halo_copies:
        copy.wait_recv()

    @pl.when(me == 0)
    def _():
        halo[0] = jnp.zeros_like(halo[0])

    @pl.when(me == n_ctx - 1)
    def _():
        halo[1] = tails[0]

    def first_group(g, _):
        rows = pl.ds(pl.multiple_of(g * FGROUP, FGROUP), FGROUP)
        conv = dot(
            jnp.concatenate([halo[0, rows, :], halo[1, rows, :]], axis=0), upper_w[g]
        )
        for b, m in enumerate(firsts):
            part = conv[b * FGROUP : (b + 1) * FGROUP] + first[b, rows, :]
            gated(rows, m, part)
        return 0

    lax.fori_loop(0, groups, first_group, 0, unroll=8)
    chunk_ends(0)
    chunk_ends(2)

    chunk_decay = jnp.exp(-rate_row * float(CHUNK))
    for b in range(2):
        end = ends[2 * b] * chunk_decay + ends[2 * b + 1]
        for h in range(2):
            for c in range(2):
                e_out[pl.ds(4 * b + 2 * h + c, 8, stride=8), :] = end[
                    8 * c : 8 * c + 8, h * LANES : (h + 1) * LANES
                ]

    def tile(n):
        if isinstance(n, int):
            return pl.ds(n * 8, 8)
        return pl.ds(pl.multiple_of(n * 8, 8), 8)

    def to_plane(source, target, send, recv):
        copies = []
        for k in range(1, RING):
            copy = pltpu.make_async_remote_copy(
                src_ref=source.at[tile(lax.rem(place + k, RING))],
                dst_ref=target.at[tile(place)],
                send_sem=send.at[k],
                recv_sem=recv.at[k],
                device_id={"ctx": in_plane(k)},
                device_id_type=MESH,
            )
            copy.start()
            copies.append(copy)
        return copies

    a_copies = to_plane(e_out, e_in, a_send, a_recv)
    e_in[tile(place), :] = e_out[tile(place), :]

    def inner_group(g, _):
        rows = pl.ds(pl.multiple_of(g * FGROUP, FGROUP), FGROUP)
        line = jnp.broadcast_to(filt[pl.ds(g, 1), :], (TAPS, CHUNK))
        skew = pltpu.roll(line, 0, 1, stride=1, stride_axis=0)
        near = jnp.where(lower_mask, skew[:, 0:TAPS], 0.0).astype(BF16)
        far = skew[:, TAPS:].astype(BF16)
        table = jnp.concatenate(
            [
                jnp.concatenate([near, far], axis=1),
                jnp.concatenate([jnp.zeros_like(near), near], axis=1),
            ],
            axis=0,
        )
        chunks = length // CHUNK
        data = [x[rows, c * CHUNK : (c + 1) * CHUNK] for c in range(chunks)]
        conv = dot(jnp.concatenate(data, axis=0), table)
        for c in range(chunks):
            y[rows, c * CHUNK : (c + 1) * CHUNK] = conv[
                c * FGROUP : (c + 1) * FGROUP
            ]
        return 0

    row = iota((8, LANES), 0)
    is_low = row < 4
    rate_tile = jnp.where(
        lax.rem(lax.div(row, 2), 2) == 0, rate_row[:, 0:LANES], rate_row[:, LANES:]
    )
    span_decay = jnp.exp(-rate_tile * float(half))
    for p in range(RING):
        count = jnp.where(is_low, p, RING - 1 - p).astype(F32)
        coef[p] = jnp.exp(-rate_tile * (half * count))
    for z in range(nz):
        count = jnp.where(is_low, plane - 1 - z, z - plane - 1)
        factor = jnp.exp(-rate_tile * (half * RING * jnp.maximum(count, 0).astype(F32)))
        coef[RING + z] = jnp.where(count >= 0, factor, 0.0)
        count = (2 * nz - 2 - z - plane).astype(F32)
        factor = jnp.exp(-rate_tile * (half * RING * count))
        coef[RING + nz + z] = jnp.where(is_low, 0.0, factor)

    lax.fori_loop(0, 6, inner_group, 0, unroll=3)

    for copy in a_copies:
        copy.wait_recv()
    state = jnp.zeros((8, LANES), F32)
    prefix = []
    for p in range(RING):
        prefix.append(state)
        state = state * span_decay + jnp.where(
            is_low, e_in[tile(p), :], e_in[tile(RING - 1 - p), :]
        )
    p_out[...] = state
    b_copies = []
    for k in range(1, nz):
        copy = pltpu.make_async_remote_copy(
            src_ref=p_out,
            dst_ref=p_in.at[tile(plane)],
            send_sem=b_send.at[k],
            recv_sem=b_recv.at[k],
            device_id={"ctx": in_column(k)},
            device_id_type=MESH,
        )
        copy.start()
        b_copies.append(copy)
    p_in[tile(plane), :] = state
    for p in range(RING):
        s_out[tile(p), :] = jnp.where(is_low, prefix[p], prefix[RING - 1 - p])

    lax.fori_loop(6, 11, inner_group, 0, unroll=5)

    for copy in b_copies:
        copy.wait_recv()
    carry = jnp.zeros((8, LANES), F32)
    for z in range(nz):
        total = p_in[tile(z), :]
        carry = carry + coef[RING + z] * total
        carry = carry + coef[RING + nz + z] * pltpu.roll(total, 4, 0)
    for p in range(RING):
        s_out[tile(p), :] = s_out[tile(p), :] + coef[p] * carry
    c_copies = to_plane(s_out, s_in, c_send, c_recv)
    s_in[tile(place), :] = s_out[tile(place), :]

    lax.fori_loop(11, groups, inner_group, 0, unroll=5)
    lq_load.wait()

    for copy in c_copies:
        copy.wait_recv()
    from_start = weight_row * jnp.exp(-rate_row)
    for b in range(2):
        for h in range(2):
            lanes = slice(h * LANES, (h + 1) * LANES)
            start = jnp.concatenate(
                [s_in[pl.ds(4 * b + 2 * h + c, 8, stride=8), :] for c in range(2)],
                axis=0,
            )
            rows = slice(h * LANES, (h + 1) * LANES)
            for c in range(2):
                chunk = 2 * b + c
                if c == 1:
                    start = start * chunk_decay[:, lanes] + ends[2 * b, :, lanes]
                scaled = start * from_start[:, lanes]
                tiled = jnp.concatenate([scaled] * (LANES // FGROUP), axis=0)
                states = jnp.where(diag, tiled, 0.0).astype(BF16)
                carried = dot_t(jnp.concatenate([states, states], axis=1), gt[h])
                cols = slice(chunk * CHUNK, (chunk + 1) * CHUNK)
                value = lq[rows, cols].astype(F32) * (y[rows, cols] + carried)
                out[rows, cols] = value.astype(BF16)

    for copy in halo_copies + a_copies + b_copies + c_copies:
        copy.wait_send()


def per_device(sq, sk, sv, lq, lk, taps, res, rate):
    chans, length = sk.shape
    n_ctx = lax.axis_size("ctx")
    nz = n_ctx // RING
    groups = chans // FGROUP
    wide = pltpu.VMEM((chans, length), BF16)
    message = pltpu.VMEM((8 * RING, LANES), F32)
    dma = pltpu.SemaphoreType.DMA
    scratch = [
        wide,
        wide,
        wide,
        wide,
        wide,
        pltpu.VMEM(taps.shape, BF16),
        pltpu.VMEM(res.shape, F32),
        pltpu.VMEM(rate.shape, F32),
        wide,
        pltpu.VMEM((2, chans, TAPS), BF16),
        pltpu.VMEM((2, chans, TAPS), BF16),
        pltpu.VMEM((2, chans, TAPS), F32),
        pltpu.VMEM((groups, TAPS, TAPS), BF16),
        pltpu.VMEM((groups, TAPS), F32),
        pltpu.VMEM((groups, groups * MODES), F32),
        pltpu.VMEM((2, CHUNK, 2 * LANES), BF16),
        pltpu.VMEM((2, CHUNK, 2 * LANES), BF16),
        pltpu.VMEM((groups, CHUNK), F32),
        wide,
        pltpu.VMEM((chans, length), F32),
        pltpu.VMEM((length // CHUNK, FGROUP, groups * MODES), F32),
        message,
        message,
        pltpu.VMEM((8, LANES), F32),
        pltpu.VMEM((8 * nz, LANES), F32),
        message,
        message,
        pltpu.VMEM((RING + 2 * nz, 8, LANES), F32),
        dma((14,)),
        dma((2,)),
        dma((2,)),
        dma((RING,)),
        dma((RING,)),
        dma((nz,)),
        dma((nz,)),
        dma((RING,)),
        dma((RING,)),
    ]
    in_hbm = pl.BlockSpec(memory_space=pltpu.HBM)
    return pl.pallas_call(
        functools.partial(kernel, n_ctx),
        out_shape=jax.ShapeDtypeStruct((chans, length), BF16),
        in_specs=[in_hbm] * 8,
        out_specs=pl.BlockSpec(memory_space=pltpu.VMEM),
        scratch_shapes=scratch,
        compiler_params=pltpu.CompilerParams(
            collective_id=0, has_side_effects=True, vmem_limit_bytes=53 << 20
        ),
    )(sq, sk, sv, lq, lk, taps, res, rate)


def solution(mesh):
    in_specs = (P("chan", "ctx"),) * 5 + (P("chan", None),) * 3
    return jax.shard_map(
        per_device,
        mesh=mesh,
        in_specs=in_specs,
        out_specs=P("chan", "ctx"),
        check_vma=False,
    )
```

time: 140 us -> 41.9 us (0.30)
  local copies, waits for them, and re-layouts: 48.9 us -> 2.87 us
  Pallas kernels: 0 us -> 38.7 us
  blocking collectives: 33.2 us -> 0 us
  starting transfers between devices: 28.9 us -> 0 us
  waiting for transfers between devices: 16.6 us -> 0 us
  other arithmetic: 7.28 us -> 0 us
  matrix products: 4.17 us -> 0 us
    pallas_call x0 -> x1, Pallas kernels: none -> 38.7 us  [per_device(): pl.pallas_call(functools.partial(kernel, n_ctx), out_shape=jax.ShapeDtype...]
    all_to_all x1 -> x0, blocking collectives: 33.2 us -> none  [per_device(): lax.all_to_all(restored, 'ctx', split_axis=1, concat_axis=0, tiled=True)]
    slice x34 -> x0, local copies, waits for them, and re-layouts: 21.6 us -> none  [the longest x27 15.7 us: block_conv(): prefix, _ = lax.associative_scan(combine, (ends, counter), axis=2)]
    ppermute x2 -> x0, starting transfers between devices: 18 us -> none  [shifted(): return lax.ppermute(shard, axis, pairs)]
    all_to_all x1 -> x0, waiting for transfers between devices: 16.6 us -> none  [per_device(): lax.all_to_all(long_input, 'ctx', split_axis=0, concat_axis=1, tiled=True)]
    all_to_all x1 -> x0, starting transfers between devices: 10.9 us -> none  [per_device(): lax.all_to_all(long_input, 'ctx', split_axis=0, concat_axis=1, tiled=True)]
    pad x14 -> x0, local copies, waits for them, and re-layouts: 7.98 us -> none  [block_conv(): prefix, _ = lax.associative_scan(combine, (ends, counter), axis=2)]
    reshape x5 -> x0, local copies, waits for them, and re-layouts: 7.41 us -> none  [the longest x3 7.05 us: skewed(): rows = tiled[:, :TAPS * (2 * TAPS - 1)].reshape(count, TAPS, 2 * TAPS - 1)]
  transfers between devices with their start and end apart: 3 -> 0, of which waited for: 1 -> 0; matrix products, arithmetic and copies ran while one was open for 9% -> 0% of each run, Pallas kernels for 0% -> 0%
where the time goes in v1:
time: 41.9 us; the launch traced here: 41.6 us
  Pallas kernels  38.7 us (92%)
  local copies, waits for them, and re-layouts  2.87 us (7%)
    pallas_call x1, Pallas kernels, per_device(): pl.pallas_call(functools.partial(kernel, n_ctx), out_shape=jax.ShapeDtype...  38.7 us
    unnamed x7, local copies, waits for them, and re-layouts  2.87 us

profile of v1, /device:TPU:1, one launch (start us, length us, event | category | flops | bytes accessed | tf_op | source)
XLA Modules:
  0.0 41.6 jit_solution(11764188075108288127)
XLA Ops:
  0.0 0.0 copy-start
  0.0 0.7 %copy-done = f32[16,16]{1,0:T(8,128)S(1)} copy-done((f32[16,16]{1,0:T(8,128)S(1)}, f32[16,16]{1,0:T(8,128)}, u32[]{:S(2)}) %copy-start) | copy-done | bytes 1048
  0.7 0.0 copy-start.1
  0.7 0.7 %copy-done.1 = f32[16,16]{1,0:T(8,128)S(1)} copy-done((f32[16,16]{1,0:T(8,128)S(1)}, f32[16,16]{1,0:T(8,128)}, u32[]{:S(2)}) %copy-start.1) | copy-done | bytes 1048
  1.4 0.0 copy-start.2
  1.4 0.7 %copy-done.2 = bf16[16,128]{1,0:T(8,128)(2,1)S(1)} copy-done((bf16[16,128]{1,0:T(8,128)(2,1)S(1)}, bf16[16,128]{1,0:T(8,128)(2,1)}, u32[]{:S(2)}) %copy-start.2) | copy-done | bytes 4120
  2.1 38.7 %shard_map.82 = bf16[256,1024]{1,0:T(8,128)(2,1)S(1)} custom-call(bf16[256,1024]{1,0:T(8,128)(2,1)} %sq_hbm.1, bf16[256,1024]{1,0:T(8,128)(2,1)} %sk_hbm.1, bf16[256,1024]{1,0:T(8,128)(2,1)} %sv_hbm.1, bf16[256,1024]{1,0:T(8,128)(2,1)} %lq_hbm.1, bf16[256,1024]{1,0:T(8,128)(2,1)} %lk_hbm.1, bf16[16,128]{1,0:T(8,128)(2,1)S(1)} %copy-done.2, ...), custom_call_target="tpu_custom_call" | custom-call | tf_op jit(solution)/shard_map/pallas_call | solution.py:465
  40.8 0.8 %copy.10 = bf16[256,1024]{1,0:T(8,128)(2,1)} copy(bf16[256,1024]{1,0:T(8,128)(2,1)S(1)} %shard_map.82) | data formatting | bytes 1048576
Async XLA Ops:
  0.0 0.7 %copy-start = (f32[16,16]{1,0:T(8,128)S(1)}, f32[16,16]{1,0:T(8,128)}, u32[]{:S(2)}) copy-start(f32[16,16]{1,0:T(8,128)} %res_hbm.1) | copy-start | bytes 3076
  0.7 0.7 %copy-start.1 = (f32[16,16]{1,0:T(8,128)S(1)}, f32[16,16]{1,0:T(8,128)}, u32[]{:S(2)}) copy-start(f32[16,16]{1,0:T(8,128)} %rate_hbm.1) | copy-start | bytes 3076
  1.4 0.7 %copy-start.2 = (bf16[16,128]{1,0:T(8,128)(2,1)S(1)}, bf16[16,128]{1,0:T(8,128)(2,1)}, u32[]{:S(2)}) copy-start(bf16[16,128]{1,0:T(8,128)(2,1)} %taps_hbm.1) | copy-start | bytes 12292

commit v2 on v1

--- a/solution.py
+++ b/solution.py
@@ -41,16 +41,14 @@
     sq_hbm,
     sk_hbm,
     sv_hbm,
-    lq_hbm,
     lk_hbm,
     taps_hbm,
     res_hbm,
     rate_hbm,
-    out,
+    conv_hbm,
     sq,
     sk,
     sv,
-    lq,
     lk,
     taps,
     res,
@@ -68,22 +66,24 @@
     x,
     y,
     ends,
-    e_out,
-    e_in,
-    p_out,
-    p_in,
-    s_out,
-    s_in,
-    coef,
+    from_z,
+    z_out,
+    z_in,
+    a_out,
+    a_in,
+    b_out,
+    b_in,
+    conv,
     load_sem,
     halo_send,
     halo_recv,
+    z_send,
+    z_recv,
     a_send,
     a_recv,
     b_send,
     b_recv,
-    c_send,
-    c_recv,
+    conv_sem,
 ):
     chans, length = sk.shape
     half = length // 2
@@ -121,7 +121,6 @@
         body_loads.append(load(8 + 2 * b, sv_hbm.at[:, lo:hi], sv.at[:, lo:hi]))
     sq_load = load(11, sq_hbm, sq)
     lk_load = load(12, lk_hbm, lk)
-    lq_load = load(13, lq_hbm, lq)
 
     barrier = pltpu.get_barrier_semaphore()
     partners = [before, after]
@@ -215,11 +214,11 @@
                 data.append(jnp.concatenate([jnp.zeros_like(here), here], axis=1))
             else:
                 data.append(mixed[rows, (m - 1) * TAPS : (m + 1) * TAPS])
-        conv = dot(
+        short = dot(
             jnp.concatenate(data, axis=0), jnp.concatenate([upper, lower], axis=0)
         )
         for m in range(blocks):
-            part = conv[m * FGROUP : (m + 1) * FGROUP]
+            part = short[m * FGROUP : (m + 1) * FGROUP]
             if m in firsts:
                 first[firsts.index(m), rows, :] = part
             else:
@@ -259,11 +258,11 @@
 
     def first_group(g, _):
         rows = pl.ds(pl.multiple_of(g * FGROUP, FGROUP), FGROUP)
-        conv = dot(
+        short = dot(
             jnp.concatenate([halo[0, rows, :], halo[1, rows, :]], axis=0), upper_w[g]
         )
         for b, m in enumerate(firsts):
-            part = conv[b * FGROUP : (b + 1) * FGROUP] + first[b, rows, :]
+            part = short[b * FGROUP : (b + 1) * FGROUP] + first[b, rows, :]
             gated(rows, m, part)
         return 0
 
@@ -272,36 +271,36 @@
     chunk_ends(2)
 
     chunk_decay = jnp.exp(-rate_row * float(CHUNK))
-    for b in range(2):
-        end = ends[2 * b] * chunk_decay + ends[2 * b + 1]
-        for h in range(2):
-            for c in range(2):
-                e_out[pl.ds(4 * b + 2 * h + c, 8, stride=8), :] = end[
-                    8 * c : 8 * c + 8, h * LANES : (h + 1) * LANES
-                ]
-
-    def tile(n):
-        if isinstance(n, int):
-            return pl.ds(n * 8, 8)
-        return pl.ds(pl.multiple_of(n * 8, 8), 8)
-
-    def to_plane(source, target, send, recv):
-        copies = []
-        for k in range(1, RING):
-            copy = pltpu.make_async_remote_copy(
-                src_ref=source.at[tile(lax.rem(place + k, RING))],
-                dst_ref=target.at[tile(place)],
-                send_sem=send.at[k],
-                recv_sem=recv.at[k],
-                device_id={"ctx": in_plane(k)},
-                device_id_type=MESH,
-            )
-            copy.start()
-            copies.append(copy)
-        return copies
-
-    a_copies = to_plane(e_out, e_in, a_send, a_recv)
-    e_in[tile(place), :] = e_out[tile(place), :]
+    end_a = ends[0] * chunk_decay + ends[1]
+    end_b = ends[2] * chunk_decay + ends[3]
+    powers = iota((RING, groups * MODES), 0).astype(F32)
+    by_block = jnp.exp(-rate_row * (powers * half))
+    powers = iota((nz, groups * MODES), 0).astype(F32)
+    by_plane = jnp.exp(-rate_row * (powers * (half * RING)))
+
+    def over_blocks(count):
+        return jnp.exp(-rate_row * (half * count.astype(F32)))
+
+    both = end_b + end_a * over_blocks(2 * n_ctx - 1 - 2 * me)
+    z_out[0] = end_a.astype(BF16)
+    z_out[1] = both.astype(BF16)
+
+    def send(source, target, k, send_sem, recv_sem, device):
+        copy = pltpu.make_async_remote_copy(
+            src_ref=source,
+            dst_ref=target.at[k],
+            send_sem=send_sem.at[k],
+            recv_sem=recv_sem.at[k],
+            device_id={"ctx": device},
+            device_id_type=MESH,
+        )
+        copy.start()
+        return copy
+
+    z_copies = [
+        send(z_out.at[lax.div(plane + k, nz)], z_in, k, z_send, z_recv, in_column(k))
+        for k in range(1, nz)
+    ]
 
     def inner_group(g, _):
         rows = pl.ds(pl.multiple_of(g * FGROUP, FGROUP), FGROUP)
@@ -318,100 +317,88 @@
         )
         chunks = length // CHUNK
         data = [x[rows, c * CHUNK : (c + 1) * CHUNK] for c in range(chunks)]
-        conv = dot(jnp.concatenate(data, axis=0), table)
+        inner = dot(jnp.concatenate(data, axis=0), table)
         for c in range(chunks):
-            y[rows, c * CHUNK : (c + 1) * CHUNK] = conv[
+            y[rows, c * CHUNK : (c + 1) * CHUNK] = inner[
                 c * FGROUP : (c + 1) * FGROUP
             ]
         return 0
 
-    row = iota((8, LANES), 0)
-    is_low = row < 4
-    rate_tile = jnp.where(
-        lax.rem(lax.div(row, 2), 2) == 0, rate_row[:, 0:LANES], rate_row[:, LANES:]
-    )
-    span_decay = jnp.exp(-rate_tile * float(half))
-    for p in range(RING):
-        count = jnp.where(is_low, p, RING - 1 - p).astype(F32)
-        coef[p] = jnp.exp(-rate_tile * (half * count))
-    for z in range(nz):
-        count = jnp.where(is_low, plane - 1 - z, z - plane - 1)
-        factor = jnp.exp(-rate_tile * (half * RING * jnp.maximum(count, 0).astype(F32)))
-        coef[RING + z] = jnp.where(count >= 0, factor, 0.0)
-        count = (2 * nz - 2 - z - plane).astype(F32)
-        factor = jnp.exp(-rate_tile * (half * RING * count))
-        coef[RING + nz + z] = jnp.where(is_low, 0.0, factor)
-
     lax.fori_loop(0, 6, inner_group, 0, unroll=3)
 
-    for copy in a_copies:
-        copy.wait_recv()
-    state = jnp.zeros((8, LANES), F32)
-    prefix = []
-    for p in range(RING):
-        prefix.append(state)
-        state = state * span_decay + jnp.where(
-            is_low, e_in[tile(p), :], e_in[tile(RING - 1 - p), :]
-        )
-    p_out[...] = state
-    b_copies = []
-    for k in range(1, nz):
-        copy = pltpu.make_async_remote_copy(
-            src_ref=p_out,
-            dst_ref=p_in.at[tile(plane)],
-            send_sem=b_send.at[k],
-            recv_sem=b_recv.at[k],
-            device_id={"ctx": in_column(k)},
-            device_id_type=MESH,
-        )
-        copy.start()
-        b_copies.append(copy)
-    p_in[tile(plane), :] = state
-    for p in range(RING):
-        s_out[tile(p), :] = jnp.where(is_low, prefix[p], prefix[RING - 1 - p])
-
-    lax.fori_loop(6, 11, inner_group, 0, unroll=5)
-
-    for copy in b_copies:
-        copy.wait_recv()
-    carry = jnp.zeros((8, LANES), F32)
-    for z in range(nz):
-        total = p_in[tile(z), :]
-        carry = carry + coef[RING + z] * total
-        carry = carry + coef[RING + nz + z] * pltpu.roll(total, 4, 0)
-    for p in range(RING):
-        s_out[tile(p), :] = s_out[tile(p), :] + coef[p] * carry
-    c_copies = to_plane(s_out, s_in, c_send, c_recv)
-    s_in[tile(place), :] = s_out[tile(place), :]
-
-    lax.fori_loop(11, groups, inner_group, 0, unroll=5)
-    lq_load.wait()
-
-    for copy in c_copies:
-        copy.wait_recv()
+    def from_planes(first_half):
+        from_z[...] = jnp.zeros_like(from_z)
+        for k in range(1, nz):
+            power = k - 1 if first_half else nz - 1 - k
+
+            @pl.when((plane >= k) if first_half else (plane < k))
+            def _():
+                z_copies[k - 1].wait_recv()
+                from_z[...] += by_plane[power : power + 1] * z_in[k].astype(F32)
+
+        return from_z[...]
+
+    one_plane = by_plane[1:2]
+    before_a = from_planes(True)
+    a_out[0] = (before_a * one_plane + end_a).astype(BF16)
+    a_out[1] = before_a.astype(BF16)
+    a_copies = [
+        send(a_out.at[lax.div(place + k, RING)], a_in, k, a_send, a_recv, in_plane(k))
+        for k in range(1, RING)
+    ]
+    before_b = from_planes(False)
+    b_out[0] = before_b.astype(BF16)
+    b_out[1] = (before_b * one_plane + both).astype(BF16)
+    b_copies = [
+        send(b_out.at[lax.div(place + k, RING)], b_in, k, b_send, b_recv, in_plane(k))
+        for k in range(1, RING)
+    ]
+
+    lax.fori_loop(6, groups, inner_group, 0, unroll=5)
+
     from_start = weight_row * jnp.exp(-rate_row)
-    for b in range(2):
+    conv_copies = []
+
+    def finish(b, start):
         for h in range(2):
             lanes = slice(h * LANES, (h + 1) * LANES)
-            start = jnp.concatenate(
-                [s_in[pl.ds(4 * b + 2 * h + c, 8, stride=8), :] for c in range(2)],
-                axis=0,
-            )
             rows = slice(h * LANES, (h + 1) * LANES)
+            state = start[:, lanes]
             for c in range(2):
                 chunk = 2 * b + c
                 if c == 1:
-                    start = start * chunk_decay[:, lanes] + ends[2 * b, :, lanes]
-                scaled = start * from_start[:, lanes]
+                    state = state * chunk_decay[:, lanes] + ends[2 * b, :, lanes]
+                scaled = state * from_start[:, lanes]
                 tiled = jnp.concatenate([scaled] * (LANES // FGROUP), axis=0)
                 states = jnp.where(diag, tiled, 0.0).astype(BF16)
                 carried = dot_t(jnp.concatenate([states, states], axis=1), gt[h])
                 cols = slice(chunk * CHUNK, (chunk + 1) * CHUNK)
-                value = lq[rows, cols].astype(F32) * (y[rows, cols] + carried)
-                out[rows, cols] = value.astype(BF16)
-
-    for copy in halo_copies + a_copies + b_copies + c_copies:
+                conv[rows, cols] = (y[rows, cols] + carried).astype(BF16)
+            cols = slice(b * half, (b + 1) * half)
+            copy = pltpu.make_async_copy(
+                conv.at[rows, cols], conv_hbm.at[rows, cols], conv_sem.at[2 * b + h]
+            )
+            copy.start()
+            conv_copies.append(copy)
+
+    start_a = before_a * by_block[RING - 1 : RING]
+    for k in range(1, RING):
+        a_copies[k - 1].wait_recv()
+        start_a = start_a + by_block[k - 1 : k] * a_in[k].astype(F32)
+    finish(0, start_a)
+
+    start_b = before_b * by_block[RING - 1 : RING] + over_blocks(
+        2 * n_ctx - 2 - 2 * me
+    ) * (start_a * by_block[1:2] + end_a)
+    for k in range(1, RING):
+        b_copies[k - 1].wait_recv()
+        start_b = start_b + by_block[RING - 1 - k : RING - k] * b_in[k].astype(F32)
+    finish(1, start_b)
+
+    for copy in halo_copies + z_copies + a_copies + b_copies:
         copy.wait_send()
+    for copy in conv_copies:
+        copy.wait()
 
 
 def per_device(sq, sk, sv, lq, lk, taps, res, rate):
@@ -419,11 +406,10 @@
     n_ctx = lax.axis_size("ctx")
     nz = n_ctx // RING
     groups = chans // FGROUP
+    states = groups * MODES
     wide = pltpu.VMEM((chans, length), BF16)
-    message = pltpu.VMEM((8 * RING, LANES), F32)
     dma = pltpu.SemaphoreType.DMA
     scratch = [
-        wide,
         wide,
         wide,
         wide,
@@ -437,41 +423,44 @@
         pltpu.VMEM((2, chans, TAPS), F32),
         pltpu.VMEM((groups, TAPS, TAPS), BF16),
         pltpu.VMEM((groups, TAPS), F32),
-        pltpu.VMEM((groups, groups * MODES), F32),
+        pltpu.VMEM((groups, states), F32),
         pltpu.VMEM((2, CHUNK, 2 * LANES), BF16),
         pltpu.VMEM((2, CHUNK, 2 * LANES), BF16),
         pltpu.VMEM((groups, CHUNK), F32),
         wide,
         pltpu.VMEM((chans, length), F32),
-        pltpu.VMEM((length // CHUNK, FGROUP, groups * MODES), F32),
-        message,
-        message,
-        pltpu.VMEM((8, LANES), F32),
-        pltpu.VMEM((8 * nz, LANES), F32),
-        message,
-        message,
-        pltpu.VMEM((RING + 2 * nz, 8, LANES), F32),
-        dma((14,)),
+        pltpu.VMEM((length // CHUNK, FGROUP, states), F32),
+        pltpu.VMEM((FGROUP, states), F32),
+        pltpu.VMEM((2, FGROUP, states), BF16),
+        pltpu.VMEM((nz, FGROUP, states), BF16),
+        pltpu.VMEM((2, FGROUP, states), BF16),
+        pltpu.VMEM((RING, FGROUP, states), BF16),
+        pltpu.VMEM((2, FGROUP, states), BF16),
+        pltpu.VMEM((RING, FGROUP, states), BF16),
+        wide,
+        dma((13,)),
         dma((2,)),
         dma((2,)),
-        dma((RING,)),
-        dma((RING,)),
         dma((nz,)),
         dma((nz,)),
         dma((RING,)),
         dma((RING,)),
+        dma((RING,)),
+        dma((RING,)),
+        dma((4,)),
     ]
-    in_hbm = pl.BlockSpec(memory_space=pltpu.HBM)
-    return pl.pallas_call(
+    anywhere = pl.BlockSpec(memory_space=pl.ANY)
+    conv = pl.pallas_call(
         functools.partial(kernel, n_ctx),
         out_shape=jax.ShapeDtypeStruct((chans, length), BF16),
-        in_specs=[in_hbm] * 8,
-        out_specs=pl.BlockSpec(memory_space=pltpu.VMEM),
+        in_specs=[anywhere] * 7,
+        out_specs=anywhere,
         scratch_shapes=scratch,
         compiler_params=pltpu.CompilerParams(
-            collective_id=0, has_side_effects=True, vmem_limit_bytes=53 << 20
+            collective_id=0, has_side_effects=True, vmem_limit_bytes=56 << 20
         ),
-    )(sq, sk, sv, lq, lk, taps, res, rate)
+    )(sq, sk, sv, lk, taps, res, rate)
+    return (lq.astype(F32) * conv.astype(F32)).astype(BF16)
 
 
 def solution(mesh):

time: 41.9 us -> 35.9 us (0.86)
  Pallas kernels: 38.7 us -> 33.6 us
  local copies, waits for them, and re-layouts: 2.87 us -> 0.01 us
  other arithmetic: 0 us -> 2.03 us
    pallas_call x1, Pallas kernels: 38.7 us -> 33.6 us  [per_device(): pl.pallas_call(functools.partial(kernel, n_ctx), out_shape=jax.ShapeDtype...]
    unnamed x7 -> x2, local copies, waits for them, and re-layouts: 2.87 us -> 0.01 us
    convert_element_type x0 -> x1, other arithmetic: none -> 2.03 us  [per_device(): return (lq.astype(F32) * conv.astype(F32)).astype(BF16)]
where the time goes in v2:
time: 35.9 us; the launch traced here: 35.6 us
  Pallas kernels  33.6 us (94%)
  other arithmetic  2.03 us (6%)
    pallas_call x1, Pallas kernels, per_device(): pl.pallas_call(functools.partial(kernel, n_ctx), out_shape=jax.ShapeDtype...  33.6 us
    convert_element_type x1, other arithmetic, per_device(): return (lq.astype(F32) * conv.astype(F32)).astype(BF16)  2.03 us

profile of v2, /device:TPU:1, one launch (start us, length us, event | category | flops | bytes accessed | tf_op | source)
XLA Modules:
  0.0 35.6 jit_solution(13989979956207038731)
XLA Ops:
  0.0 0.0 copy-start
  0.0 33.6 %shard_map.82 = bf16[256,1024]{1,0:T(8,128)(2,1)} custom-call(bf16[256,1024]{1,0:T(8,128)(2,1)} %sq_hbm.1, bf16[256,1024]{1,0:T(8,128)(2,1)} %sk_hbm.1, bf16[256,1024]{1,0:T(8,128)(2,1)} %sv_hbm.1, bf16[256,1024]{1,0:T(8,128)(2,1)} %lk_hbm.1, bf16[16,128]{1,0:T(8,128)(2,1)} %taps_hbm.1, f32[16,16]{1,0:T(8,128)} %res_hbm.1, f32[16,16]{1,0:T(8,128)} %rate_hbm.1), custom_call_target="tpu_custom_call" | custom-call | tf_op jit(solution)/shard_map/pallas_call | solution.py:453
  33.6 0.0 copy-done
  33.6 2.0 %multiply_convert_fusion = bf16[256,1024]{1,0:T(8,128)(2,1)} fusion(bf16[256,1024]{1,0:T(8,128)(2,1)} %shard_map.82, bf16[256,1024]{1,0:T(8,128)(2,1)S(1)} %copy-done), kind=kLoop, calls=%fused_computation | loop fusion | flops 1048576 | bytes 1572864 | tf_op jit(solution)/shard_map/convert_element_type | solution.py:463
Async XLA Ops:
  0.0 33.6 %copy-start = (bf16[256,1024]{1,0:T(8,128)(2,1)S(1)}, bf16[256,1024]{1,0:T(8,128)(2,1)}, u32[]{:S(2)}) copy-start(bf16[256,1024]{1,0:T(8,128)(2,1)} %param.11) | copy-start | bytes 1572868

commit v3 on v2

--- a/solution.py
+++ b/solution.py
@@ -41,22 +41,25 @@
     sq_hbm,
     sk_hbm,
     sv_hbm,
+    lq_hbm,
     lk_hbm,
     taps_hbm,
-    res_hbm,
-    rate_hbm,
-    conv_hbm,
+    modes_hbm,
+    out,
     sq,
     sk,
     sv,
+    lq,
     lk,
     taps,
-    res,
-    rate,
+    modes,
     mixed,
     tails,
     halo,
     first,
+    gates,
+    added,
+    relay,
     upper_w,
     taps_f,
     pad,
@@ -73,7 +76,7 @@
     a_in,
     b_out,
     b_in,
-    conv,
+    v_in,
     load_sem,
     halo_send,
     halo_recv,
@@ -83,7 +86,13 @@
     a_recv,
     b_send,
     b_recv,
-    conv_sem,
+    relay_send,
+    relay_recv,
+    v_send,
+    v_recv,
+    up,
+    go,
+    wrap,
 ):
     chans, length = sk.shape
     half = length // 2
@@ -108,28 +117,70 @@
 
     tail_cols = ((half - TAPS, half), (length - TAPS, length))
     body_cols = ((0, half - TAPS), (half, length - TAPS))
-    tail_loads = []
-    for b, (lo, hi) in enumerate(tail_cols):
-        tail_loads.append(load(2 * b, sk_hbm.at[:, lo:hi], sk.at[:, lo:hi]))
-        tail_loads.append(load(2 * b + 1, sv_hbm.at[:, lo:hi], sv.at[:, lo:hi]))
-    rate_load = load(4, rate_hbm, rate)
-    res_load = load(5, res_hbm, res)
-    taps_load = load(6, taps_hbm, taps)
-    body_loads = []
-    for b, (lo, hi) in enumerate(body_cols):
-        body_loads.append(load(7 + 2 * b, sk_hbm.at[:, lo:hi], sk.at[:, lo:hi]))
-        body_loads.append(load(8 + 2 * b, sv_hbm.at[:, lo:hi], sv.at[:, lo:hi]))
-    sq_load = load(11, sq_hbm, sq)
-    lk_load = load(12, lk_hbm, lk)
+    gate_cols = ((0, TAPS), (half, half + TAPS))
+    rest_cols = ((TAPS, half), (half + TAPS, length))
+
+    def load_pairs(n, pairs, columns):
+        copies = []
+        for lo, hi in columns:
+            for src, dst in pairs:
+                copies.append(load(n + len(copies), src.at[:, lo:hi], dst.at[:, lo:hi]))
+        return copies
+
+    mixed_pair = ((sk_hbm, sk), (sv_hbm, sv))
+    gate_pair = ((sq_hbm, sq), (lk_hbm, lk))
+    tail_loads = load_pairs(0, mixed_pair, tail_cols)
+    gate_loads = load_pairs(4, gate_pair, gate_cols)
+    modes_load = load(8, modes_hbm, modes)
+    taps_load = load(9, taps_hbm, taps)
+    body_loads = load_pairs(11, mixed_pair, body_cols)
+    rest_loads = load_pairs(15, gate_pair, rest_cols)
+    lq_load = load(10, lq_hbm, lq)
+
+    hub = RING // 2 - 1
+    border = nz - place
+    both_true = jnp.logical_and
+    negate = jnp.logical_not
+    is_first = me == 0
+    is_last = me == n_ctx - 1
+    at_hub = place == hub
+    inner_place = both_true(place >= 2, place < nz)
+    at_relay = both_true(plane == 0, inner_place)
+    top_edge = both_true(place == RING - 1, both_true(plane >= 1, plane < nz - 1))
+    low_edge = both_true(place == 0, plane >= 2)
+    edge = jnp.logical_or(top_edge, low_edge)
 
     barrier = pltpu.get_barrier_semaphore()
-    partners = [before, after]
-    partners += [in_plane(k) for k in range(1, RING)]
-    partners += [in_column(k) for k in range(1, nz)]
-    for partner in partners:
+
+    def signal(semaphore, device):
         pl.semaphore_signal(
-            barrier, inc=1, device_id={"ctx": partner}, device_id_type=MESH
-        )
+            semaphore, inc=1, device_id={"ctx": device}, device_id_type=MESH
+        )
+
+    pl.when(negate(jnp.logical_or(is_first, low_edge)))(lambda: signal(barrier, before))
+    pl.when(negate(is_last))(lambda: signal(barrier, after))
+    pl.when(negate(at_hub))(lambda: signal(barrier, plane * RING + hub))
+
+    @pl.when(at_hub)
+    def _():
+        for k in range(1, RING):
+            signal(barrier, in_plane(k))
+
+    for k in range(1, nz):
+        pl.when(plane + k < nz)(functools.partial(signal, barrier, in_column(k)))
+
+    @pl.when(at_relay)
+    def _():
+        signal(barrier, border * RING + RING - 1)
+        signal(barrier, border * RING + RING)
+
+    greetings = (
+        negate(is_first).astype(jnp.int32)
+        + negate(jnp.logical_or(is_last, top_edge)).astype(jnp.int32)
+        + jnp.where(at_hub, RING - 1, 1)
+        + plane
+        + edge.astype(jnp.int32)
+    )
 
     for copy in tail_loads:
         copy.wait()
@@ -137,7 +188,7 @@
         product = sk[:, lo:hi] * sv[:, lo:hi]
         mixed[:, lo:hi] = product
         tails[b] = product
-    pl.semaphore_wait(barrier, len(partners))
+    pl.semaphore_wait(barrier, greetings)
 
     halo_copies = []
     for b, target in enumerate((after, before)):
@@ -149,12 +200,53 @@
             device_id={"ctx": target},
             device_id_type=MESH,
         )
-        copy.start()
         halo_copies.append(copy)
-
-    rate_load.wait()
-    res_load.wait()
+    pl.when(negate(jnp.logical_or(is_last, top_edge)))(halo_copies[0].start)
+    pl.when(negate(is_first))(halo_copies[1].start)
+
+    pl.when(low_edge)(lambda: signal(wrap, before))
+    for k in range(1, nz):
+        pl.when(plane >= k)(functools.partial(signal, up.at[k], in_column(nz - k)))
+
+    @pl.when(at_hub)
+    def _():
+        for k in range(1, RING):
+            signal(go, in_plane(k))
+
+    for copy in gate_loads:
+        copy.wait()
+    for b, (lo, hi) in enumerate(gate_cols):
+        gates[b] = sq[:, lo:hi] * lk[:, lo:hi]
+
+    def to_relay(n, source, device):
+        return pltpu.make_async_remote_copy(
+            src_ref=source,
+            dst_ref=relay.at[n],
+            send_sem=relay_send.at[n],
+            recv_sem=relay_recv.at[n],
+            device_id={"ctx": device},
+            device_id_type=MESH,
+        )
+
+    top_device = lax.rem(nz - plane, nz)
+    top_copies = [
+        to_relay(0, tails.at[0], top_device),
+        to_relay(1, gates.at[1], top_device),
+    ]
+    low_device = lax.rem(nz - plane + 1, nz)
+    low_copies = [
+        to_relay(2, gates.at[0], low_device),
+        to_relay(3, tails.at[1], low_device),
+    ]
+    for copy in top_copies:
+        pl.when(top_edge)(copy.start)
+    for copy in low_copies:
+        pl.when(low_edge)(copy.start)
+
+    modes_load.wait()
     taps_load.wait()
+    rate = modes[0:groups, :]
+    res = modes[groups : 2 * groups, :]
     taps_f[...] = taps[...].astype(F32)
 
     def spread(values):
@@ -162,8 +254,8 @@
         pad[:, 0:MODES] = values
         return pltpu.roll(pad[...], 0, 1, stride=MODES, stride_axis=0)
 
-    rate_row = jnp.sum(spread(rate[...]), axis=0, keepdims=True)
-    weight = spread(res[...] * jnp.sqrt(rate[...]))
+    rate_row = jnp.sum(spread(rate), axis=0, keepdims=True)
+    weight = spread(res * jnp.sqrt(rate))
     weight_row = jnp.sum(weight, axis=0, keepdims=True)
     steps = iota((CHUNK, LANES), 0).astype(F32)
     for h in range(2):
@@ -188,8 +280,8 @@
         copy.wait()
     for lo, hi in body_cols:
         mixed[:, lo:hi] = sk[:, lo:hi] * sv[:, lo:hi]
-    sq_load.wait()
-    lk_load.wait()
+    for copy in rest_loads:
+        copy.wait()
 
     lower_mask = iota((TAPS, TAPS), 1) >= iota((TAPS, TAPS), 0)
     blocks = length // TAPS
@@ -221,8 +313,7 @@
             part = short[m * FGROUP : (m + 1) * FGROUP]
             if m in firsts:
                 first[firsts.index(m), rows, :] = part
-            else:
-                gated(rows, m, part)
+            gated(rows, m, part)
         return 0
 
     lax.fori_loop(0, groups, short_group, 0, unroll=4)
@@ -242,37 +333,10 @@
                 own.reshape(LANES // FGROUP, FGROUP, LANES), axis=0
             )
 
-    chunk_ends(1)
-    chunk_ends(3)
-
-    for copy in halo_copies:
-        copy.wait_recv()
-
-    @pl.when(me == 0)
-    def _():
-        halo[0] = jnp.zeros_like(halo[0])
-
-    @pl.when(me == n_ctx - 1)
-    def _():
-        halo[1] = tails[0]
-
-    def first_group(g, _):
-        rows = pl.ds(pl.multiple_of(g * FGROUP, FGROUP), FGROUP)
-        short = dot(
-            jnp.concatenate([halo[0, rows, :], halo[1, rows, :]], axis=0), upper_w[g]
-        )
-        for b, m in enumerate(firsts):
-            part = short[b * FGROUP : (b + 1) * FGROUP] + first[b, rows, :]
-            gated(rows, m, part)
-        return 0
-
-    lax.fori_loop(0, groups, first_group, 0, unroll=8)
-    chunk_ends(0)
-    chunk_ends(2)
+    for chunk in range(length // CHUNK):
+        chunk_ends(chunk)
 
     chunk_decay = jnp.exp(-rate_row * float(CHUNK))
-    end_a = ends[0] * chunk_decay + ends[1]
-    end_b = ends[2] * chunk_decay + ends[3]
     powers = iota((RING, groups * MODES), 0).astype(F32)
     by_block = jnp.exp(-rate_row * (powers * half))
     powers = iota((nz, groups * MODES), 0).astype(F32)
@@ -281,12 +345,20 @@
     def over_blocks(count):
         return jnp.exp(-rate_row * (half * count.astype(F32)))
 
-    both = end_b + end_a * over_blocks(2 * n_ctx - 1 - 2 * me)
-    z_out[0] = end_a.astype(BF16)
-    z_out[1] = both.astype(BF16)
+    between = over_blocks(2 * n_ctx - 1 - 2 * me)
+
+    def first_ends(values):
+        parts = []
+        for h in range(2):
+            wide = dot(values[h * LANES : (h + 1) * LANES, :], fe[h, 0:TAPS, :])
+            own = jnp.where(diag, wide[:, 0:LANES] + wide[:, LANES:], 0.0)
+            parts.append(
+                jnp.sum(own.reshape(LANES // FGROUP, FGROUP, LANES), axis=0)
+            )
+        return jnp.concatenate(parts, axis=1)
 
     def send(source, target, k, send_sem, recv_sem, device):
-        copy = pltpu.make_async_remote_copy(
+        return pltpu.make_async_remote_copy(
             src_ref=source,
             dst_ref=target.at[k],
             send_sem=send_sem.at[k],
@@ -294,13 +366,85 @@
             device_id={"ctx": device},
             device_id_type=MESH,
         )
-        copy.start()
-        return copy
-
-    z_copies = [
-        send(z_out.at[lax.div(plane + k, nz)], z_in, k, z_send, z_recv, in_column(k))
-        for k in range(1, nz)
-    ]
+
+    z_copies = []
+    is_down = []
+    is_early = []
+    for k in range(1, nz):
+        down = plane + k >= nz
+        early = both_true(edge, down)
+        if k == nz - 1:
+            early = both_true(early, negate(low_edge))
+        kind = jnp.where(down, jnp.where(early, 2, 1), 0)
+        z_copies.append(send(z_out.at[kind], z_in, k, z_send, z_recv, in_column(k)))
+        is_down.append(down)
+        is_early.append(early)
+
+    def block_ends():
+        end_a = ends[0] * chunk_decay + ends[1]
+        end_b = ends[2] * chunk_decay + ends[3]
+        return end_a, end_b + end_a * between
+
+    @pl.when(is_first)
+    def _():
+        halo[0] = jnp.zeros_like(halo[0])
+
+    @pl.when(is_last)
+    def _():
+        halo[1] = tails[0]
+
+    def add_halo(b):
+        away = jnp.logical_or(both_true(b == 0, is_first), both_true(b == 1, is_last))
+        copy = pltpu.make_async_remote_copy(
+            src_ref=tails.at[b],
+            dst_ref=halo.at[b],
+            send_sem=halo_send.at[b],
+            recv_sem=halo_recv.at[b],
+            device_id={"ctx": after},
+            device_id_type=MESH,
+        )
+        pl.when(negate(away))(copy.wait_recv)
+        cols = pl.ds(pl.multiple_of(b * half, TAPS), TAPS)
+
+        def group(g, _):
+            rows = pl.ds(pl.multiple_of(g * FGROUP, FGROUP), FGROUP)
+            extra = dot(halo[b, rows, :], upper_w[g])
+            query = sq[rows, cols].astype(F32)
+            key = lk[rows, cols].astype(F32)
+            added[0, rows, :] = (key * (query * extra)).astype(BF16)
+            x[rows, cols] = (key * (query * (extra + first[b, rows, :]))).astype(BF16)
+            return 0
+
+        lax.fori_loop(0, groups, group, 0, unroll=8)
+        ends[2 * b] += first_ends(added[0])
+
+    near = jnp.where(place == 0, 1, 0)
+    add_halo(near)
+
+    @pl.when(edge)
+    def _():
+        z_out[2] = block_ends()[1].astype(BF16)
+        for k in range(1, nz):
+            pl.when(is_early[k - 1])(z_copies[k - 1].start)
+
+    @pl.when(top_edge)
+    def _():
+        pl.semaphore_wait(wrap, 1)
+        halo_copies[0].start()
+
+    add_halo(1 - near)
+    end_a, both = block_ends()
+    z_out[0] = end_a.astype(BF16)
+    z_out[1] = both.astype(BF16)
+    for k in range(1, nz):
+        late = both_true(is_down[k - 1], negate(is_early[k - 1]))
+        pl.when(late)(z_copies[k - 1].start)
+    for k in range(1, nz):
+
+        @pl.when(negate(is_down[k - 1]))
+        def _():
+            pl.semaphore_wait(up.at[k], 1)
+            z_copies[k - 1].start()
 
     def inner_group(g, _):
         rows = pl.ds(pl.multiple_of(g * FGROUP, FGROUP), FGROUP)
@@ -336,6 +480,14 @@
                 z_copies[k - 1].wait_recv()
                 from_z[...] += by_plane[power : power + 1] * z_in[k].astype(F32)
 
+        if not first_half:
+
+            @pl.when(both_true(inner_place, plane < border))
+            def _():
+                pl.when(plane >= 1)(v_copies[0].wait_recv)
+                count = jnp.maximum(RING * (border - plane) - 1 - place, 0)
+                from_z[...] += over_blocks(count) * v_in[...].astype(F32)
+
         return from_z[...]
 
     one_plane = by_plane[1:2]
@@ -346,6 +498,44 @@
         send(a_out.at[lax.div(place + k, RING)], a_in, k, a_send, a_recv, in_plane(k))
         for k in range(1, RING)
     ]
+    pl.when(negate(at_hub))(lambda: pl.semaphore_wait(go, 1))
+    for copy in a_copies:
+        copy.start()
+
+    v_copies = [
+        pltpu.make_async_remote_copy(
+            src_ref=v_in,
+            dst_ref=v_in,
+            send_sem=v_send.at[k],
+            recv_sem=v_recv,
+            device_id={"ctx": in_column(k)},
+            device_id_type=MESH,
+        )
+        for k in range(1, nz - 1)
+    ]
+
+    @pl.when(at_relay)
+    def _():
+        for n in range(4):
+            to_relay(n, relay.at[n], top_device).wait_recv()
+
+        def group(g, _):
+            rows = pl.ds(pl.multiple_of(g * FGROUP, FGROUP), FGROUP)
+            ended = jnp.concatenate([relay[0, rows, :], relay[3, rows, :]], axis=0)
+            extra = dot(ended, upper_w[g])
+            for b in range(2):
+                part = extra[b * FGROUP : (b + 1) * FGROUP]
+                gate = relay[2 - b, rows, :].astype(F32)
+                added[b, rows, :] = (gate * part).astype(BF16)
+            return 0
+
+        lax.fori_loop(0, groups, group, 0, unroll=8)
+        far = over_blocks(2 * RING * (place - 1))
+        state = first_ends(added[1]) + first_ends(added[0]) * far
+        v_in[...] = (state * chunk_decay).astype(BF16)
+        for k in range(1, nz - 1):
+            pl.when(k < border)(v_copies[k - 1].start)
+
     before_b = from_planes(False)
     b_out[0] = before_b.astype(BF16)
     b_out[1] = (before_b * one_plane + both).astype(BF16)
@@ -353,11 +543,13 @@
         send(b_out.at[lax.div(place + k, RING)], b_in, k, b_send, b_recv, in_plane(k))
         for k in range(1, RING)
     ]
+    for copy in b_copies:
+        copy.start()
 
     lax.fori_loop(6, groups, inner_group, 0, unroll=5)
 
     from_start = weight_row * jnp.exp(-rate_row)
-    conv_copies = []
+    lq_load.wait()
 
     def finish(b, start):
         for h in range(2):
@@ -373,13 +565,8 @@
                 states = jnp.where(diag, tiled, 0.0).astype(BF16)
                 carried = dot_t(jnp.concatenate([states, states], axis=1), gt[h])
                 cols = slice(chunk * CHUNK, (chunk + 1) * CHUNK)
-                conv[rows, cols] = (y[rows, cols] + carried).astype(BF16)
-            cols = slice(b * half, (b + 1) * half)
-            copy = pltpu.make_async_copy(
-                conv.at[rows, cols], conv_hbm.at[rows, cols], conv_sem.at[2 * b + h]
-            )
-            copy.start()
-            conv_copies.append(copy)
+                value = lq[rows, cols].astype(F32) * (y[rows, cols] + carried)
+                out[rows, cols] = value.astype(BF16)
 
     start_a = before_a * by_block[RING - 1 : RING]
     for k in range(1, RING):
@@ -395,10 +582,16 @@
         start_b = start_b + by_block[RING - 1 - k : RING - k] * b_in[k].astype(F32)
     finish(1, start_b)
 
-    for copy in halo_copies + z_copies + a_copies + b_copies:
+    pl.when(negate(is_last))(halo_copies[0].wait_send)
+    pl.when(negate(is_first))(halo_copies[1].wait_send)
+    for copy in top_copies:
+        pl.when(top_edge)(copy.wait_send)
+    for copy in low_copies:
+        pl.when(low_edge)(copy.wait_send)
+    for k in range(1, nz - 1):
+        pl.when(both_true(at_relay, k < border))(v_copies[k - 1].wait_send)
+    for copy in z_copies + a_copies + b_copies:
         copy.wait_send()
-    for copy in conv_copies:
-        copy.wait()
 
 
 def per_device(sq, sk, sv, lq, lk, taps, res, rate):
@@ -414,13 +607,16 @@
         wide,
         wide,
         wide,
+        wide,
         pltpu.VMEM(taps.shape, BF16),
-        pltpu.VMEM(res.shape, F32),
-        pltpu.VMEM(rate.shape, F32),
+        pltpu.VMEM((2 * groups, MODES), F32),
         wide,
         pltpu.VMEM((2, chans, TAPS), BF16),
         pltpu.VMEM((2, chans, TAPS), BF16),
         pltpu.VMEM((2, chans, TAPS), F32),
+        pltpu.VMEM((2, chans, TAPS), BF16),
+        pltpu.VMEM((2, chans, TAPS), BF16),
+        pltpu.VMEM((4, chans, TAPS), BF16),
         pltpu.VMEM((groups, TAPS, TAPS), BF16),
         pltpu.VMEM((groups, TAPS), F32),
         pltpu.VMEM((groups, states), F32),
@@ -431,14 +627,14 @@
         pltpu.VMEM((chans, length), F32),
         pltpu.VMEM((length // CHUNK, FGROUP, states), F32),
         pltpu.VMEM((FGROUP, states), F32),
-        pltpu.VMEM((2, FGROUP, states), BF16),
+        pltpu.VMEM((3, FGROUP, states), BF16),
         pltpu.VMEM((nz, FGROUP, states), BF16),
         pltpu.VMEM((2, FGROUP, states), BF16),
         pltpu.VMEM((RING, FGROUP, states), BF16),
         pltpu.VMEM((2, FGROUP, states), BF16),
         pltpu.VMEM((RING, FGROUP, states), BF16),
-        wide,
-        dma((13,)),
+        pltpu.VMEM((FGROUP, states), BF16),
+        dma((19,)),
         dma((2,)),
         dma((2,)),
         dma((nz,)),
@@ -448,19 +644,25 @@
         dma((RING,)),
         dma((RING,)),
         dma((4,)),
+        dma((4,)),
+        dma((nz,)),
+        dma(()),
+        pltpu.SemaphoreType.REGULAR((nz,)),
+        pltpu.SemaphoreType.REGULAR,
+        pltpu.SemaphoreType.REGULAR,
     ]
     anywhere = pl.BlockSpec(memory_space=pl.ANY)
-    conv = pl.pallas_call(
+    modes = jnp.concatenate([rate, res], axis=0)
+    return pl.pallas_call(
         functools.partial(kernel, n_ctx),
         out_shape=jax.ShapeDtypeStruct((chans, length), BF16),
         in_specs=[anywhere] * 7,
-        out_specs=anywhere,
+        out_specs=pl.BlockSpec(memory_space=pltpu.VMEM),
         scratch_shapes=scratch,
         compiler_params=pltpu.CompilerParams(
-            collective_id=0, has_side_effects=True, vmem_limit_bytes=56 << 20
+            collective_id=0, has_side_effects=True, vmem_limit_bytes=53 << 20
         ),
-    )(sq, sk, sv, lk, taps, res, rate)
-    return (lq.astype(F32) * conv.astype(F32)).astype(BF16)
+    )(sq, sk, sv, lq, lk, taps, modes)
 
 
 def solution(mesh):

time: 35.9 us -> 33.1 us (0.922)
  Pallas kernels: 33.6 us -> 31.4 us
  other arithmetic: 2.03 us -> 0.73 us
  local copies, waits for them, and re-layouts: 0.01 us -> 0.8 us
    pallas_call x1, Pallas kernels: 33.6 us -> 31.4 us  [per_device(): pl.pallas_call(functools.partial(kernel, n_ctx), out_shape=jax.ShapeDtype...]
    convert_element_type x1 -> x0, other arithmetic: 2.03 us -> none  [per_device(): return (lq.astype(F32) * conv.astype(F32)).astype(BF16)]
    unnamed x2 -> x3, local copies, waits for them, and re-layouts: 0.01 us -> 0.8 us
    concatenate x0 -> x1, other arithmetic: none -> 0.73 us  [per_device(): modes = jnp.concatenate([rate, res], axis=0)]
where the time goes in v3:
time: 33.1 us; the launch traced here: 32.9 us
  Pallas kernels  31.4 us (95%)
  local copies, waits for them, and re-layouts  0.8 us (2%)
  other arithmetic  0.73 us (2%)
    pallas_call x1, Pallas kernels, per_device(): pl.pallas_call(functools.partial(kernel, n_ctx), out_shape=jax.ShapeDtype...  31.4 us
    unnamed x3, local copies, waits for them, and re-layouts  0.8 us
    concatenate x1, other arithmetic, per_device(): modes = jnp.concatenate([rate, res], axis=0)  0.73 us

profile of v3, /device:TPU:1, one launch (start us, length us, event | category | flops | bytes accessed | tf_op | source)
XLA Modules:
  0.0 32.9 jit_solution(10546887635637743818)
XLA Ops:
  0.0 0.0 copy-start
  0.0 0.7 %pad_maximum_fusion.modes_hbm = f32[32,16]{1,0:T(8,128)S(1)} fusion(f32[16,16]{1,0:T(8,128)} %param.14, f32[16,16]{1,0:T(8,128)} %param.15), kind=kLoop, calls=%fused_computation | loop fusion | flops 512 | bytes 4096 | tf_op jit(solution)/shard_map/concatenate | solution.py:655
  0.7 0.0 copy-done
  0.7 31.4 %shard_map.82 = bf16[256,1024]{1,0:T(8,128)(2,1)S(1)} custom-call(bf16[256,1024]{1,0:T(8,128)(2,1)} %sq_hbm.1, bf16[256,1024]{1,0:T(8,128)(2,1)} %sk_hbm.1, bf16[256,1024]{1,0:T(8,128)(2,1)} %sv_hbm.1, bf16[256,1024]{1,0:T(8,128)(2,1)} %lq_hbm.1, bf16[256,1024]{1,0:T(8,128)(2,1)} %lk_hbm.1, bf16[16,128]{1,0:T(8,128)(2,1)S(1)} %copy-done, ...), custom_call_target="tpu_custom_call" | custom-call | tf_op jit(solution)/shard_map/pallas_call | solution.py:656
  32.1 0.8 %copy.10 = bf16[256,1024]{1,0:T(8,128)(2,1)} copy(bf16[256,1024]{1,0:T(8,128)(2,1)S(1)} %shard_map.82) | data formatting | bytes 1048576
Async XLA Ops:
  0.0 0.7 %copy-start = (bf16[16,128]{1,0:T(8,128)(2,1)S(1)}, bf16[16,128]{1,0:T(8,128)(2,1)}, u32[]{:S(2)}) copy-start(bf16[16,128]{1,0:T(8,128)(2,1)} %taps_hbm.1) | copy-start | bytes 12292

commit v4 on v3

--- a/solution.py
+++ b/solution.py
@@ -150,6 +150,16 @@
     low_edge = both_true(place == 0, plane >= 2)
     edge = jnp.logical_or(top_edge, low_edge)
 
+    is_late_column = both_true(lax.axis_index("chan") == 0, place == 0)
+    is_late = both_true(is_late_column, plane == 0)
+    is_known = []
+    for k in range(1, nz):
+        other = lax.rem(plane + k, nz)
+        other_late = both_true(is_late_column, other == 0)
+        known = jnp.logical_or(both_true(other < plane, negate(other_late)), is_late)
+        is_known.append(known)
+    entered = sum(known.astype(jnp.int32) for known in is_known)
+
     barrier = pltpu.get_barrier_semaphore()
 
     def signal(semaphore, device):
@@ -161,13 +171,10 @@
     pl.when(negate(is_last))(lambda: signal(barrier, after))
     pl.when(negate(at_hub))(lambda: signal(barrier, plane * RING + hub))
 
-    @pl.when(at_hub)
-    def _():
-        for k in range(1, RING):
-            signal(barrier, in_plane(k))
-
     for k in range(1, nz):
-        pl.when(plane + k < nz)(functools.partial(signal, barrier, in_column(k)))
+        pl.when(negate(is_known[k - 1]))(
+            functools.partial(signal, barrier, in_column(k))
+        )
 
     @pl.when(at_relay)
     def _():
@@ -177,8 +184,8 @@
     greetings = (
         negate(is_first).astype(jnp.int32)
         + negate(jnp.logical_or(is_last, top_edge)).astype(jnp.int32)
-        + jnp.where(at_hub, RING - 1, 1)
-        + plane
+        + jnp.where(at_hub, RING - 1, 0)
+        + entered
         + edge.astype(jnp.int32)
     )
 
@@ -206,7 +213,9 @@
 
     pl.when(low_edge)(lambda: signal(wrap, before))
     for k in range(1, nz):
-        pl.when(plane >= k)(functools.partial(signal, up.at[k], in_column(nz - k)))
+        pl.when(is_known[nz - k - 1])(
+            functools.partial(signal, up.at[k], in_column(nz - k))
+        )
 
     @pl.when(at_hub)
     def _():
@@ -415,17 +424,25 @@
             x[rows, cols] = (key * (query * (extra + first[b, rows, :]))).astype(BF16)
             return 0
 
-        lax.fori_loop(0, groups, group, 0, unroll=8)
+        lax.fori_loop(0, groups, group, 0, unroll=16)
         ends[2 * b] += first_ends(added[0])
 
-    near = jnp.where(place == 0, 1, 0)
+    near = 1 - lax.rem(place, 2)
     add_halo(near)
+
+    def start_column(k, wanted):
+        @pl.when(wanted)
+        def _():
+            pl.when(negate(is_known[k - 1]))(lambda: pl.semaphore_wait(up.at[k], 1))
+            z_copies[k - 1].start()
 
     @pl.when(edge)
     def _():
         z_out[2] = block_ends()[1].astype(BF16)
         for k in range(1, nz):
-            pl.when(is_early[k - 1])(z_copies[k - 1].start)
+            start_column(k, both_true(is_early[k - 1], is_known[k - 1]))
+        for k in range(1, nz):
+            start_column(k, both_true(is_early[k - 1], negate(is_known[k - 1])))
 
     @pl.when(top_edge)
     def _():
@@ -438,13 +455,9 @@
     z_out[1] = both.astype(BF16)
     for k in range(1, nz):
         late = both_true(is_down[k - 1], negate(is_early[k - 1]))
-        pl.when(late)(z_copies[k - 1].start)
+        start_column(k, late)
     for k in range(1, nz):
-
-        @pl.when(negate(is_down[k - 1]))
-        def _():
-            pl.semaphore_wait(up.at[k], 1)
-            z_copies[k - 1].start()
+        start_column(k, negate(is_down[k - 1]))
 
     def inner_group(g, _):
         rows = pl.ds(pl.multiple_of(g * FGROUP, FGROUP), FGROUP)
@@ -529,7 +542,7 @@
                 added[b, rows, :] = (gate * part).astype(BF16)
             return 0
 
-        lax.fori_loop(0, groups, group, 0, unroll=8)
+        lax.fori_loop(0, groups, group, 0, unroll=16)
         far = over_blocks(2 * RING * (place - 1))
         state = first_ends(added[1]) + first_ends(added[0]) * far
         v_in[...] = (state * chunk_decay).astype(BF16)

time: 33.1 us -> 32.6 us (0.985)
  Pallas kernels: 31.4 us -> 30.9 us
    pallas_call x1, Pallas kernels: 31.4 us -> 30.9 us  [per_device(): pl.pallas_call(functools.partial(kernel, n_ctx), out_shape=jax.ShapeDtype...]
where the time goes in v4:
time: 32.6 us; the launch traced here: 32.4 us
  Pallas kernels  30.9 us (95%)
  local copies, waits for them, and re-layouts  0.8 us (2%)
  other arithmetic  0.73 us (2%)
    pallas_call x1, Pallas kernels, per_device(): pl.pallas_call(functools.partial(kernel, n_ctx), out_shape=jax.ShapeDtype...  30.9 us
    unnamed x3, local copies, waits for them, and re-layouts  0.8 us
    concatenate x1, other arithmetic, per_device(): modes = jnp.concatenate([rate, res], axis=0)  0.73 us

profile of v4, /device:TPU:1, one launch (start us, length us, event | category | flops | bytes accessed | tf_op | source)
XLA Modules:
  0.0 32.4 jit_solution(4200451829907281837)
XLA Ops:
  0.0 0.0 copy-start
  0.0 0.7 %pad_maximum_fusion.modes_hbm = f32[32,16]{1,0:T(8,128)S(1)} fusion(f32[16,16]{1,0:T(8,128)} %param.14, f32[16,16]{1,0:T(8,128)} %param.15), kind=kLoop, calls=%fused_computation | loop fusion | flops 512 | bytes 4096 | tf_op jit(solution)/shard_map/concatenate | solution.py:668
  0.7 0.0 copy-done
  0.7 30.9 %shard_map.82 = bf16[256,1024]{1,0:T(8,128)(2,1)S(1)} custom-call(bf16[256,1024]{1,0:T(8,128)(2,1)} %sq_hbm.1, bf16[256,1024]{1,0:T(8,128)(2,1)} %sk_hbm.1, bf16[256,1024]{1,0:T(8,128)(2,1)} %sv_hbm.1, bf16[256,1024]{1,0:T(8,128)(2,1)} %lq_hbm.1, bf16[256,1024]{1,0:T(8,128)(2,1)} %lk_hbm.1, bf16[16,128]{1,0:T(8,128)(2,1)S(1)} %copy-done, ...), custom_call_target="tpu_custom_call" | custom-call | tf_op jit(solution)/shard_map/pallas_call | solution.py:669
  31.7 0.8 %copy.10 = bf16[256,1024]{1,0:T(8,128)(2,1)} copy(bf16[256,1024]{1,0:T(8,128)(2,1)S(1)} %shard_map.82) | data formatting | bytes 1048576
Async XLA Ops:
  0.0 0.7 %copy-start = (bf16[16,128]{1,0:T(8,128)(2,1)S(1)}, bf16[16,128]{1,0:T(8,128)(2,1)}, u32[]{:S(2)}) copy-start(bf16[16,128]{1,0:T(8,128)(2,1)} %taps_hbm.1) | copy-start | bytes 12292

commit v5 on v4

--- a/solution.py
+++ b/solution.py
@@ -93,6 +93,8 @@
     up,
     go,
     wrap,
+    hand,
+    up_near,
 ):
     chans, length = sk.shape
     half = length // 2
@@ -149,6 +151,7 @@
     top_edge = both_true(place == RING - 1, both_true(plane >= 1, plane < nz - 1))
     low_edge = both_true(place == 0, plane >= 2)
     edge = jnp.logical_or(top_edge, low_edge)
+    low_hand = both_true(place == 0, both_true(plane >= 1, plane < nz - 1))
 
     is_late_column = both_true(lax.axis_index("chan") == 0, place == 0)
     is_late = both_true(is_late_column, plane == 0)
@@ -168,7 +171,7 @@
         )
 
     pl.when(negate(jnp.logical_or(is_first, low_edge)))(lambda: signal(barrier, before))
-    pl.when(negate(is_last))(lambda: signal(barrier, after))
+    pl.when(negate(jnp.logical_or(is_last, top_edge)))(lambda: signal(barrier, after))
     pl.when(negate(at_hub))(lambda: signal(barrier, plane * RING + hub))
 
     for k in range(1, nz):
@@ -182,12 +185,45 @@
         signal(barrier, border * RING + RING)
 
     greetings = (
-        negate(is_first).astype(jnp.int32)
+        negate(jnp.logical_or(is_first, low_edge)).astype(jnp.int32)
         + negate(jnp.logical_or(is_last, top_edge)).astype(jnp.int32)
         + jnp.where(at_hub, RING - 1, 0)
         + entered
         + edge.astype(jnp.int32)
     )
+
+    modes_load.wait()
+    taps_load.wait()
+    rate = modes[0:groups, :]
+    res = modes[groups : 2 * groups, :]
+    taps_f[...] = taps[...].astype(F32)
+
+    def spread(values):
+        pad[...] = jnp.zeros_like(pad)
+        pad[:, 0:MODES] = values
+        return pltpu.roll(pad[...], 0, 1, stride=MODES, stride_axis=0)
+
+    rate_row = jnp.sum(spread(rate), axis=0, keepdims=True)
+    weight = spread(res * jnp.sqrt(rate))
+    weight_row = jnp.sum(weight, axis=0, keepdims=True)
+    steps = iota((CHUNK, LANES), 0).astype(F32)
+    for h in range(2):
+        r = rate_row[:, h * LANES : (h + 1) * LANES]
+        high, low = split_float(jnp.exp(-r * steps))
+        gt[h, :, 0:LANES] = high
+        gt[h, :, LANES:] = low
+        high, low = split_float(jnp.exp(-r * (CHUNK - 1.0 - steps)))
+        fe[h, :, 0:LANES] = high
+        fe[h, :, LANES:] = low
+
+    total = jnp.zeros((groups, CHUNK), F32)
+    for h in range(2):
+        high, low = split_float(weight[:, h * LANES : (h + 1) * LANES])
+        total = total + dot_t(jnp.concatenate([high, high], axis=1), gt[h])
+        total = total + dot_t(
+            jnp.concatenate([low, jnp.zeros_like(low)], axis=1), gt[h]
+        )
+    filt[...] = total
 
     for copy in tail_loads:
         copy.wait()
@@ -209,13 +245,14 @@
         )
         halo_copies.append(copy)
     pl.when(negate(jnp.logical_or(is_last, top_edge)))(halo_copies[0].start)
-    pl.when(negate(is_first))(halo_copies[1].start)
-
-    pl.when(low_edge)(lambda: signal(wrap, before))
+    pl.when(negate(jnp.logical_or(is_first, low_edge)))(halo_copies[1].start)
+
     for k in range(1, nz):
         pl.when(is_known[nz - k - 1])(
             functools.partial(signal, up.at[k], in_column(nz - k))
         )
+
+    pl.when(low_edge)(lambda: signal(up_near, in_column(nz - 1)))
 
     @pl.when(at_hub)
     def _():
@@ -251,39 +288,6 @@
         pl.when(top_edge)(copy.start)
     for copy in low_copies:
         pl.when(low_edge)(copy.start)
-
-    modes_load.wait()
-    taps_load.wait()
-    rate = modes[0:groups, :]
-    res = modes[groups : 2 * groups, :]
-    taps_f[...] = taps[...].astype(F32)
-
-    def spread(values):
-        pad[...] = jnp.zeros_like(pad)
-        pad[:, 0:MODES] = values
-        return pltpu.roll(pad[...], 0, 1, stride=MODES, stride_axis=0)
-
-    rate_row = jnp.sum(spread(rate), axis=0, keepdims=True)
-    weight = spread(res * jnp.sqrt(rate))
-    weight_row = jnp.sum(weight, axis=0, keepdims=True)
-    steps = iota((CHUNK, LANES), 0).astype(F32)
-    for h in range(2):
-        r = rate_row[:, h * LANES : (h + 1) * LANES]
-        high, low = split_float(jnp.exp(-r * steps))
-        gt[h, :, 0:LANES] = high
-        gt[h, :, LANES:] = low
-        high, low = split_float(jnp.exp(-r * (CHUNK - 1.0 - steps)))
-        fe[h, :, 0:LANES] = high
-        fe[h, :, LANES:] = low
-
-    total = jnp.zeros((groups, CHUNK), F32)
-    for h in range(2):
-        high, low = split_float(weight[:, h * LANES : (h + 1) * LANES])
-        total = total + dot_t(jnp.concatenate([high, high], axis=1), gt[h])
-        total = total + dot_t(
-            jnp.concatenate([low, jnp.zeros_like(low)], axis=1), gt[h]
-        )
-    filt[...] = total
 
     for copy in body_loads:
         copy.wait()
@@ -444,6 +448,19 @@
         for k in range(1, nz):
             start_column(k, both_true(is_early[k - 1], negate(is_known[k - 1])))
 
+    pl.when(low_hand)(lambda: pl.semaphore_wait(go, 1))
+
+    @pl.when(low_hand)
+    def _():
+        pl.semaphore_wait(up_near, 1)
+        signal(hand, in_column(1))
+
+    @pl.when(low_edge)
+    def _():
+        pl.semaphore_wait(hand, 1)
+        signal(wrap, before)
+        halo_copies[1].start()
+
     @pl.when(top_edge)
     def _():
         pl.semaphore_wait(wrap, 1)
@@ -483,23 +500,26 @@
 
     lax.fori_loop(0, 6, inner_group, 0, unroll=3)
 
+    relay_decay = over_blocks(
+        jnp.maximum(RING * (border - plane) - 1 - place, 0)
+    )
+
     def from_planes(first_half):
         from_z[...] = jnp.zeros_like(from_z)
-        for k in range(1, nz):
+        if not first_half:
+
+            @pl.when(both_true(inner_place, plane < border))
+            def _():
+                pl.when(plane >= 1)(v_copies[0].wait_recv)
+                from_z[...] += relay_decay * v_in[...].astype(F32)
+
+        for k in reversed(range(1, nz)):
             power = k - 1 if first_half else nz - 1 - k
 
             @pl.when((plane >= k) if first_half else (plane < k))
             def _():
                 z_copies[k - 1].wait_recv()
                 from_z[...] += by_plane[power : power + 1] * z_in[k].astype(F32)
-
-        if not first_half:
-
-            @pl.when(both_true(inner_place, plane < border))
-            def _():
-                pl.when(plane >= 1)(v_copies[0].wait_recv)
-                count = jnp.maximum(RING * (border - plane) - 1 - place, 0)
-                from_z[...] += over_blocks(count) * v_in[...].astype(F32)
 
         return from_z[...]
 
@@ -511,7 +531,9 @@
         send(a_out.at[lax.div(place + k, RING)], a_in, k, a_send, a_recv, in_plane(k))
         for k in range(1, RING)
     ]
-    pl.when(negate(at_hub))(lambda: pl.semaphore_wait(go, 1))
+    pl.when(negate(jnp.logical_or(at_hub, low_hand)))(
+        lambda: pl.semaphore_wait(go, 1)
+    )
     for copy in a_copies:
         copy.start()
 
@@ -663,6 +685,8 @@
         pltpu.SemaphoreType.REGULAR((nz,)),
         pltpu.SemaphoreType.REGULAR,
         pltpu.SemaphoreType.REGULAR,
+        pltpu.SemaphoreType.REGULAR,
+        pltpu.SemaphoreType.REGULAR,
     ]
     anywhere = pl.BlockSpec(memory_space=pl.ANY)
     modes = jnp.concatenate([rate, res], axis=0)

time: 32.6 us -> 32.2 us (0.988)
  Pallas kernels: 30.9 us -> 30.5 us
    pallas_call x1, Pallas kernels: 30.9 us -> 30.5 us  [per_device(): pl.pallas_call(functools.partial(kernel, n_ctx), out_shape=jax.ShapeDtype...]
where the time goes in v5:
time: 32.2 us; the launch traced here: 32 us
  Pallas kernels  30.5 us (95%)
  local copies, waits for them, and re-layouts  0.8 us (2%)
  other arithmetic  0.73 us (2%)
    pallas_call x1, Pallas kernels, per_device(): pl.pallas_call(functools.partial(kernel, n_ctx), out_shape=jax.ShapeDtype...  30.5 us
    unnamed x3, local copies, waits for them, and re-layouts  0.8 us
    concatenate x1, other arithmetic, per_device(): modes = jnp.concatenate([rate, res], axis=0)  0.73 us

profile of v5, /device:TPU:1, one launch (start us, length us, event | category | flops | bytes accessed | tf_op | source)
XLA Modules:
  0.0 32.0 jit_solution(7270766238853046611)
XLA Ops:
  0.0 0.0 copy-start
  0.0 0.7 %pad_maximum_fusion.modes_hbm = f32[32,16]{1,0:T(8,128)S(1)} fusion(f32[16,16]{1,0:T(8,128)} %param.14, f32[16,16]{1,0:T(8,128)} %param.15), kind=kLoop, calls=%fused_computation | loop fusion | flops 512 | bytes 4096 | tf_op jit(solution)/shard_map/concatenate | solution.py:692
  0.7 0.0 copy-done
  0.7 30.5 %shard_map.82 = bf16[256,1024]{1,0:T(8,128)(2,1)S(1)} custom-call(bf16[256,1024]{1,0:T(8,128)(2,1)} %sq_hbm.1, bf16[256,1024]{1,0:T(8,128)(2,1)} %sk_hbm.1, bf16[256,1024]{1,0:T(8,128)(2,1)} %sv_hbm.1, bf16[256,1024]{1,0:T(8,128)(2,1)} %lq_hbm.1, bf16[256,1024]{1,0:T(8,128)(2,1)} %lk_hbm.1, bf16[16,128]{1,0:T(8,128)(2,1)S(1)} %copy-done, ...), custom_call_target="tpu_custom_call" | custom-call | tf_op jit(solution)/shard_map/pallas_call | solution.py:693
  31.2 0.8 %copy.10 = bf16[256,1024]{1,0:T(8,128)(2,1)} copy(bf16[256,1024]{1,0:T(8,128)(2,1)S(1)} %shard_map.82) | data formatting | bytes 1048576
Async XLA Ops:
  0.0 0.7 %copy-start = (bf16[16,128]{1,0:T(8,128)(2,1)S(1)}, bf16[16,128]{1,0:T(8,128)(2,1)}, u32[]{:S(2)}) copy-start(bf16[16,128]{1,0:T(8,128)(2,1)} %taps_hbm.1) | copy-start | bytes 12292

commit v6 on v5

--- a/solution.py
+++ b/solution.py
@@ -61,6 +61,7 @@
     added,
     relay,
     upper_w,
+    lower_w,
     taps_f,
     pad,
     fe,
@@ -135,8 +136,11 @@
     gate_loads = load_pairs(4, gate_pair, gate_cols)
     modes_load = load(8, modes_hbm, modes)
     taps_load = load(9, taps_hbm, taps)
-    body_loads = load_pairs(11, mixed_pair, body_cols)
-    rest_loads = load_pairs(15, gate_pair, rest_cols)
+    block_loads = []
+    for b in range(2):
+        pairs = load_pairs(11 + 4 * b, mixed_pair, body_cols[b : b + 1])
+        pairs += load_pairs(13 + 4 * b, gate_pair, rest_cols[b : b + 1])
+        block_loads.append(pairs)
     lq_load = load(10, lq_hbm, lq)
 
     hub = RING // 2 - 1
@@ -289,13 +293,6 @@
     for copy in low_copies:
         pl.when(low_edge)(copy.start)
 
-    for copy in body_loads:
-        copy.wait()
-    for lo, hi in body_cols:
-        mixed[:, lo:hi] = sk[:, lo:hi] * sv[:, lo:hi]
-    for copy in rest_loads:
-        copy.wait()
-
     lower_mask = iota((TAPS, TAPS), 1) >= iota((TAPS, TAPS), 0)
     blocks = length // TAPS
     firsts = (0, blocks // 2)
@@ -305,31 +302,41 @@
         value = lk[rows, cols].astype(F32) * (sq[rows, cols].astype(F32) * conv)
         x[rows, cols] = value.astype(BF16)
 
-    def short_group(g, _):
+    def short_group(b, g, _):
         rows = pl.ds(pl.multiple_of(g * FGROUP, FGROUP), FGROUP)
-        line = jnp.broadcast_to(taps_f[pl.ds(g, 1), :], (TAPS, TAPS))
-        skew = pltpu.roll(line, 0, 1, stride=1, stride_axis=0)
-        upper = jnp.where(lower_mask, 0.0, skew).astype(BF16)
-        lower = jnp.where(lower_mask, skew, 0.0).astype(BF16)
-        upper_w[g] = upper
-        data = []
-        for m in range(blocks):
-            if m in firsts:
-                here = mixed[rows, m * TAPS : (m + 1) * TAPS]
-                data.append(jnp.concatenate([jnp.zeros_like(here), here], axis=1))
-            else:
-                data.append(mixed[rows, (m - 1) * TAPS : (m + 1) * TAPS])
+        if b == 0:
+            line = jnp.broadcast_to(taps_f[pl.ds(g, 1), :], (TAPS, TAPS))
+            skew = pltpu.roll(line, 0, 1, stride=1, stride_axis=0)
+            upper = jnp.where(lower_mask, 0.0, skew).astype(BF16)
+            lower = jnp.where(lower_mask, skew, 0.0).astype(BF16)
+            upper_w[g] = upper
+            lower_w[g] = lower
+        else:
+            upper = upper_w[g]
+            lower = lower_w[g]
+        begin = firsts[b]
+        end = begin + blocks // 2
+        here = mixed[rows, begin * TAPS : (begin + 1) * TAPS]
+        data = [jnp.concatenate([jnp.zeros_like(here), here], axis=1)]
+        for m in range(begin + 1, end):
+            data.append(mixed[rows, (m - 1) * TAPS : (m + 1) * TAPS])
         short = dot(
             jnp.concatenate(data, axis=0), jnp.concatenate([upper, lower], axis=0)
         )
-        for m in range(blocks):
-            part = short[m * FGROUP : (m + 1) * FGROUP]
-            if m in firsts:
-                first[firsts.index(m), rows, :] = part
+        for m in range(begin, end):
+            part = short[(m - begin) * FGROUP : (m - begin + 1) * FGROUP]
+            if m == begin:
+                first[b, rows, :] = part
             gated(rows, m, part)
         return 0
 
-    lax.fori_loop(0, groups, short_group, 0, unroll=4)
+    for b, (lo, hi) in enumerate(body_cols):
+        for copy in block_loads[b]:
+            copy.wait()
+        mixed[:, lo:hi] = sk[:, lo:hi] * sv[:, lo:hi]
+        lax.fori_loop(
+            0, groups, functools.partial(short_group, b), 0, unroll=8
+        )
 
     diag = lax.div(iota((LANES, LANES), 0), FGROUP) == lax.div(
         iota((LANES, LANES), 1), MODES
@@ -652,6 +659,7 @@
         pltpu.VMEM((2, chans, TAPS), BF16),
         pltpu.VMEM((2, chans, TAPS), BF16),
         pltpu.VMEM((4, chans, TAPS), BF16),
+        pltpu.VMEM((groups, TAPS, TAPS), BF16),
         pltpu.VMEM((groups, TAPS, TAPS), BF16),
         pltpu.VMEM((groups, TAPS), F32),
         pltpu.VMEM((groups, states), F32),

time: 32.2 us -> 32.2 us (level)
  no operation moved by 1% of the time
where the time goes in v6:
time: 32.2 us; the launch traced here: 32 us
  Pallas kernels  30.5 us (95%)
  local copies, waits for them, and re-layouts  0.8 us (2%)
  other arithmetic  0.73 us (2%)
    pallas_call x1, Pallas kernels, per_device(): pl.pallas_call(functools.partial(kernel, n_ctx), out_shape=jax.ShapeDtype...  30.5 us
    unnamed x3, local copies, waits for them, and re-layouts  0.8 us
    concatenate x1, other arithmetic, per_device(): modes = jnp.concatenate([rate, res], axis=0)  0.73 us

profile of v6, /device:TPU:1, one launch (start us, length us, event | category | flops | bytes accessed | tf_op | source)
XLA Modules:
  0.0 32.0 jit_solution(6261029628237291776)
XLA Ops:
  0.0 0.0 copy-start
  0.0 0.7 %pad_maximum_fusion.modes_hbm = f32[32,16]{1,0:T(8,128)S(1)} fusion(f32[16,16]{1,0:T(8,128)} %param.14, f32[16,16]{1,0:T(8,128)} %param.15), kind=kLoop, calls=%fused_computation | loop fusion | flops 512 | bytes 4096 | tf_op jit(solution)/shard_map/concatenate | solution.py:700
  0.7 0.0 copy-done
  0.7 30.5 %shard_map.82 = bf16[256,1024]{1,0:T(8,128)(2,1)S(1)} custom-call(bf16[256,1024]{1,0:T(8,128)(2,1)} %sq_hbm.1, bf16[256,1024]{1,0:T(8,128)(2,1)} %sk_hbm.1, bf16[256,1024]{1,0:T(8,128)(2,1)} %sv_hbm.1, bf16[256,1024]{1,0:T(8,128)(2,1)} %lq_hbm.1, bf16[256,1024]{1,0:T(8,128)(2,1)} %lk_hbm.1, bf16[16,128]{1,0:T(8,128)(2,1)S(1)} %copy-done, ...), custom_call_target="tpu_custom_call" | custom-call | tf_op jit(solution)/shard_map/pallas_call | solution.py:701
  31.2 0.8 %copy.10 = bf16[256,1024]{1,0:T(8,128)(2,1)} copy(bf16[256,1024]{1,0:T(8,128)(2,1)S(1)} %shard_map.82) | data formatting | bytes 1048576
Async XLA Ops:
  0.0 0.7 %copy-start = (bf16[16,128]{1,0:T(8,128)(2,1)S(1)}, bf16[16,128]{1,0:T(8,128)(2,1)}, u32[]{:S(2)}) copy-start(bf16[16,128]{1,0:T(8,128)(2,1)} %taps_hbm.1) | copy-start | bytes 12292
